TPU v7x, 32 devices: a whole 2x2x4 slice. The times are simulated.
32 devices in a mesh: seq: 2 (over x), row: 16 (over z, y, core).
Axes of the slice: x: 2, y: 2, z: 4, core: 2. Of those that a mesh axis runs over, the one named last changes fastest.
Arguments:
- qm: float32 [2, 16, 7, 256, 256], P('seq', 'row'), parts along dimension 0, may hold values from 0.005 to 0.05
- qm1: float32 [2, 16, 7, 256, 256], P('seq', 'row'), parts along dimension 0, may hold values from 0.005 to 0.05
- qb: float32 [2, 16, 7, 256, 256], P('seq', 'row'), parts along dimension 0, may hold values from 0.05 to 2
- codes: int32 [2, 16, 256], P('seq', 'row'), parts along dimension 0, may hold values from 0 to 3
- energy_index: int32 [2, 16, 256, 256], P('seq', 'row'), parts along dimension 0, may hold values from 0 to 63
- turner: float32 [64], replicated, may hold values from -1 to 1.5
Outputs:
- qb_new: float32 [2, 16, 256, 256], P('seq', 'row'), parts along dimension 0
- qm1_new: float32 [2, 16, 256, 256], P('seq', 'row'), parts along dimension 0
- qm_new: float32 [2, 16, 256, 256], P('seq', 'row'), parts along dimension 0
There are 2 independent parts, one for each index of `seq`. A program takes and returns all parts, laid end to end along the dimension named above; an argument that names none is the same for every part. Nothing has to cross between parts.
All inputs are finite; a program needn't handle non-finite values.
Results may differ from a plain program's by a relative error of at most 0.0003.
Values sent between devices are 32-bit elements; how exact they have to be, the bound alone decides.
No kernel may reach another device: no remote copies, remote signals or barrier semaphores. Data moves between devices by JAX's collectives and lax.ppermute only.
A program may use at most 64 MiB of HBM per device.

v0:
```python
import jax
import jax.numpy as jnp
import numpy as np
from jax import lax
from jax.sharding import PartitionSpec as P

B = 256
DIST = 8


PAIRS = np.array([[0, 0, 0, 1], [0, 0, 1, 0], [0, 1, 0, 1], [1, 0, 1, 0]], dtype=np.float32)
HI = lax.Precision.HIGHEST


def shifted(block, axis, distance):
    devices = range(lax.axis_size(axis))
    route = [((i - distance) % len(devices), i) for i in devices]
    return lax.ppermute(block, axis, route)


def unpaired(shift):
    offsets = jnp.arange(B, dtype=jnp.int32)
    diffs = (shift * B + offsets[None, :] - offsets[:, None]).astype(jnp.float32)
    values = 0.01 * jnp.exp(-diffs / (DIST * B))
    if shift == 0:
        values = jnp.where(diffs >= 0, values, jnp.float32(0.0))
    return values


def decay(level):
    offsets = jnp.arange(B, dtype=jnp.int32)
    diffs = ((DIST - level) * B + offsets[None, :] - offsets[:, None]).astype(jnp.float32)
    values = jnp.exp(-diffs / (DIST * B))
    if level == DIST:
        values = jnp.where(diffs >= 0, values, jnp.float32(0.0))
    return values


def pairing(first, second):
    table = jnp.asarray(PAIRS, dtype=jnp.float32)
    digits = jnp.arange(4, dtype=jnp.int32)
    left = (first[:, None] == digits[None, :]).astype(jnp.float32)
    right = (second[:, None] == digits[None, :]).astype(jnp.float32)
    return jnp.dot(jnp.dot(left, table, precision=HI), right.T, precision=HI)


def per_device(qm, qm1, qb, codes, energy_index, turner):
    width = lax.axis_size("row")
    myself = lax.axis_index("row")
    cycles = qm.shape[0]
    qm = qm[:, 0]
    qm1 = qm1[:, 0]
    qb = qb[:, 0]
    codes = codes[:, 0]
    energy_index = energy_index[:, 0]
    beta = 1.0 / (DIST * B)

    def advance(received, step):
        later = jnp.concatenate([received[1:], jnp.zeros_like(received)], 0)
        return jnp.where(myself + step >= width, later, received)

    rights = []
    for shift in range(1, DIST):
        piece = shifted(qm1[:, DIST - shift - 1], "row", -shift)
        rights.append(advance(piece, shift))
    ends = advance(shifted(codes, "row", -DIST), DIST)
    start_tail = unpaired(0)
    closing_decay = decay(DIST)
    live = 0 + myself + DIST < cycles * width
    allowed = pairing(codes[0], ends[0])
    weight = jnp.exp(-jnp.take(turner, energy_index[0]))
    summed = jnp.zeros((B, B), jnp.float32)
    for shift in range(1, DIST):
        summed = summed + jnp.dot(qm[0, shift - 1], rights[shift - 1][0], precision=HI)
    pair_new = allowed * weight * (1.0 + 0.8 * summed)
    branch = jnp.dot(pair_new, closing_decay, precision=HI)
    tails = jnp.zeros((B, B), jnp.float32)
    for shift in range(1, DIST):
        tails = tails + jnp.dot(unpaired(shift), rights[shift - 1][0], precision=HI)
    for level in range(1, DIST):
        branch = branch + jnp.dot(qb[0, level - 1], decay(level), precision=HI)
    branch = branch * beta
    multi = summed + tails + jnp.dot(start_tail, branch, precision=HI)
    zero = jnp.float32(0.0)
    pair_out = [jnp.where(live, pair_new, zero)]
    branch_out = [jnp.where(live, branch, zero)]
    multi_out = [jnp.where(live, multi, zero)]
    return (
        jnp.stack(pair_out, 0)[:, None],
        jnp.stack(branch_out, 0)[:, None],
        jnp.stack(multi_out, 0)[:, None],
    )


def solution(mesh):
    return jax.shard_map(
        per_device,
        mesh=mesh,
        in_specs=(
            P("seq", "row", None, None, None),
            P("seq", "row", None, None, None),
            P("seq", "row", None, None, None),
            P("seq", "row", None),
            P("seq", "row", None, None),
            P(),
        ),
        out_specs=(
            P("seq", "row", None, None),
            P("seq", "row", None, None),
            P("seq", "row", None, None),
        ),
        check_vma=False,
    )
```

profile of v0, /device:TPU:0, one launch (start us, length us, event | category | flops | bytes accessed | tf_op | source)
XLA Modules:
  0.0 712.9 jit_solution(10599824790510033032)
XLA Ops:
  0.6 0.0 copy-start
  0.7 0.0 copy-start.8
  0.7 2.7 slice_bitcast_fusion.34
  3.4 3.5 collective-permute-start.7
  6.9 1.5 collective-permute-start.6
  8.4 3.3 collective-permute-start.5
  11.7 1.3 collective-permute-start.4
  13.1 0.6 iota_add_fusion.6
  13.7 0.6 iota_add_fusion.5
  14.3 0.6 iota_add_fusion.4
  14.9 0.6 iota_add_fusion.3
  15.5 0.1 copy.52
  15.7 0.9 fusion.131
  16.7 0.0 copy-start.2
  16.7 668.8 %gather_fusion = f32[65536]{0:T(1024)} fusion(f32[64]{0:T(128)S(1)} %copy-done, s32[65536]{0:T(1024)S(1)} %broadcast_clamp_fusion), kind=kCustom, calls=%fused_computation | custom fusion | bytes 786432 | tf_op jit(solution)/shard_map/jit(_take)/gather | solution.py:71
  685.5 1.0 reshape.78
  686.6 2.2 collective-permute-start.3
  688.8 0.7 broadcast_select_fusion
  689.5 0.4 fusion.25
  689.9 3.7 collective-permute-start.1
  693.6 0.4 fusion.26
  694.0 0.4 fusion.27
  694.4 0.4 fusion.28
  694.8 1.0 collective-permute-done.3
  695.8 0.4 fusion.29
  696.2 4.1 collective-permute-done.2
  700.3 0.4 fusion.30
  700.7 0.0 copy-start.1
  700.8 2.4 collective-permute-done.1
  703.1 0.4 fusion.15
  703.6 0.4 fusion.10
  704.0 0.4 fusion.61
  704.4 0.4 fusion.8
  704.9 0.4 fusion.7
  705.4 0.4 fusion.6
  705.8 0.4 fusion.5
  706.3 0.4 fusion.4
  706.7 0.4 fusion.3
  707.2 0.4 fusion.2
  707.6 0.5 fusion.51
  708.1 0.8 select_bitcast_fusion
  708.9 0.4 fusion.31
  709.4 0.4 fusion.34
  709.8 0.4 fusion.37
  710.3 0.4 fusion.40
  710.7 0.4 fusion.43
  711.2 0.4 fusion.46
  711.6 1.2 fusion.23
  (26 shorter events, 0.1 us)
Async XLA Ops:
  0.6 16.0 %copy-start = (f32[64]{0:T(128)S(1)}, f32[64]{0:T(128)}, u32[]{:S(2)}) copy-start(f32[64]{0:T(128)} %param.12) | copy-start | bytes 772
  0.6 14.8 %copy-start.3 = (s32[1,1,256,256]{3,2,1,0:T(8,128)S(1)}, s32[1,1,256,256]{3,2,1,0:T(8,128)}, u32[]{:S(2)}) copy-start(s32[1,1,256,256]{3,2,1,0:T(8,128)} %param.11) | copy-start | bytes 786436
  0.7 15.0 %copy-start.8 = (f32[4,4]{1,0:T(4,128)S(1)}, f32[4,4]{1,0:T(4,128)}, u32[]{:S(2)}) copy-start(f32[4,4]{1,0:T(4,128)} %constant.76.clone) | copy-start | bytes 196
  3.4 686.1 %collective-permute-start.7 = (f32[1,256,256]{2,1,0:T(8,128)}, f32[1,256,256]{2,1,0:T(8,128)S(1)}, u32[]{:S(2)}, u32[]{:S(2)}) collective-permute-start(f32[1,256,256]{2,1,0:T(8,128)} %get-tuple-element.4), channel_id=1, source_target_pairs={{7,0},{8,1},{9,2},{10,3},{11,4},{12,5},{13,6},{14,7},{15,8},{0,9},... | collective-permute-start | bytes 786440 | tf_op jit(solution)/shard_map/ppermute | solution.py:18
  6.9 683.0 %collective-permute-start.6 = (f32[1,256,256]{2,1,0:T(8,128)}, f32[1,256,256]{2,1,0:T(8,128)S(1)}, u32[]{:S(2)}, u32[]{:S(2)}) collective-permute-start(f32[1,256,256]{2,1,0:T(8,128)} %get-tuple-element.5), channel_id=1, source_target_pairs={{6,0},{7,1},{8,2},{9,3},{10,4},{11,5},{12,6},{13,7},{14,8},{15,9},... | collective-permute-start | bytes 786440 | tf_op jit(solution)/shard_map/ppermute | solution.py:18
  8.4 685.6 %collective-permute-start.5 = (f32[1,256,256]{2,1,0:T(8,128)}, f32[1,256,256]{2,1,0:T(8,128)S(1)}, u32[]{:S(2)}, u32[]{:S(2)}) collective-permute-start(f32[1,256,256]{2,1,0:T(8,128)} %get-tuple-element.6), channel_id=1, source_target_pairs={{5,0},{6,1},{7,2},{8,3},{9,4},{10,5},{11,6},{12,7},{13,8},{14,9},{... | collective-permute-start | bytes 786440 | tf_op jit(solution)/shard_map/ppermute | solution.py:18
  11.7 682.7 %collective-permute-start.4 = (f32[1,256,256]{2,1,0:T(8,128)}, f32[1,256,256]{2,1,0:T(8,128)S(1)}, u32[]{:S(2)}, u32[]{:S(2)}) collective-permute-start(f32[1,256,256]{2,1,0:T(8,128)} %get-tuple-element.7), channel_id=1, source_target_pairs={{4,0},{5,1},{6,2},{7,3},{8,4},{9,5},{10,6},{11,7},{12,8},{13,9},{1... | collective-permute-start | bytes 786440 | tf_op jit(solution)/shard_map/ppermute | solution.py:18
  13.1 673.4 %collective-permute-start = (s32[1,256]{1,0:T(1,128)}, s32[1,256]{1,0:T(1,128)}, u32[]{:S(2)}, u32[]{:S(2)}) collective-permute-start(s32[1,256]{1,0:T(1,128)} %bitcast.1), channel_id=1, source_target_pairs={{8,0},{9,1},{10,2},{11,3},{12,4},{13,5},{14,6},{15,7},{0,8},{1,9},... | collective-permute-start | bytes 3080 | tf_op jit(solution)/shard_map/ppermute | solution.py:18
  16.7 672.8 %copy-start.2 = (f32[1,1,7,256,256]{4,3,2,1,0:T(8,128)S(1)}, f32[1,1,7,256,256]{4,3,2,1,0:T(8,128)}, u32[]{:S(2)}) copy-start(f32[1,1,7,256,256]{4,3,2,1,0:T(8,128)} %param.7) | copy-start | bytes 5505028
  686.6 9.3 %collective-permute-start.3 = (f32[1,256,256]{2,1,0:T(8,128)}, f32[1,256,256]{2,1,0:T(8,128)S(1)}, u32[]{:S(2)}, u32[]{:S(2)}) collective-permute-start(f32[1,256,256]{2,1,0:T(8,128)} %get-tuple-element.8), channel_id=1, source_target_pairs={{3,0},{4,1},{5,2},{6,3},{7,4},{8,5},{9,6},{10,7},{11,8},{12,9},{13... | collective-permute-start | bytes 786440 | tf_op jit(solution)/shard_map/ppermute | solution.py:18
  689.5 10.8 %collective-permute-start.2 = (f32[1,256,256]{2,1,0:T(8,128)}, f32[1,256,256]{2,1,0:T(8,128)S(1)}, u32[]{:S(2)}, u32[]{:S(2)}) collective-permute-start(f32[1,256,256]{2,1,0:T(8,128)} %get-tuple-element.9), channel_id=1, source_target_pairs={{2,0},{3,1},{4,2},{5,3},{6,4},{7,5},{8,6},{9,7},{10,8},{11,9},{12,... | collective-permute-start | bytes 786440 | tf_op jit(solution)/shard_map/ppermute | solution.py:18
  689.9 13.2 %collective-permute-start.1 = (f32[1,256,256]{2,1,0:T(8,128)}, f32[1,256,256]{2,1,0:T(8,128)S(1)}, u32[]{:S(2)}, u32[]{:S(2)}) collective-permute-start(f32[1,256,256]{2,1,0:T(8,128)} %get-tuple-element.3), channel_id=1, source_target_pairs={{1,0},{2,1},{3,2},{4,3},{5,4},{6,5},{7,6},{8,7},{9,8},{10,9},{11,1... | collective-permute-start | bytes 786440 | tf_op jit(solution)/shard_map/ppermute | solution.py:18
  700.7 3.7 copy-start.1
  700.7 3.7 copy-start.7
  703.6 1.3 copy-start.6
  703.6 1.8 copy-start.5
  703.6 2.2 copy-start.4
where the time goes:
time: 713 us
  local copies, waits for them, and re-layouts  673 us (94%)
  starting transfers between devices  15.6 us (2%)
  matrix products  12 us (2%)
  waiting for transfers between devices  7.48 us (1%)
    gather x2, local copies, waits for them, and re-layouts, per_device(): weight = jnp.exp(-jnp.take(turner, energy_index[0]))  670 us
    ppermute x8, starting transfers between devices, shifted(): return lax.ppermute(block, axis, route)  15.6 us
  transfers between devices with their start and end apart: 8, of which 3 were waited for; matrix products, arithmetic and copies ran while one was open for 95% of the time, Pallas kernels for 0%

commit v1 on v0

v1 whole, which is shorter than its diff:
```python
import functools

import jax
import jax.numpy as jnp
from jax import lax
from jax.experimental import pallas as pl
from jax.experimental.pallas import tpu as pltpu
from jax.sharding import PartitionSpec as P

F32 = jnp.float32
BF16 = jnp.bfloat16
LANES = 128


def halves(x):
    high = x.astype(BF16)
    return high, (x - high.astype(F32)).astype(BF16)


def dot(a, b):
    return jnp.dot(a, b, preferred_element_type=F32)


def product(left, right):
    left_high, left_low = halves(left)
    right_high, right_low = halves(right)
    return dot(left_high, right_high) + dot(left_high, right_low) + dot(left_low, right_high)


def column(size, start, beta):
    steps = lax.broadcasted_iota(jnp.int32, (size, 1), 0) + start
    return jnp.exp(steps.astype(F32) * -beta)


def row(size, start, beta):
    steps = lax.broadcasted_iota(jnp.int32, (1, size), 1) + start
    return jnp.exp(steps.astype(F32) * -beta)


def weights_kernel(dist, index_ref, turner_ref, qb_ref, weight_ref, branch_ref):
    size = index_ref.shape[0]
    beta = 1.0 / (dist * size)
    entries = turner_ref.shape[1]
    for start in range(0, size, LANES):
        index = index_ref[:, start:start + LANES]
        found = jnp.zeros(index.shape, F32)
        for first in range(0, entries, LANES):
            table = jnp.exp(-turner_ref[:, first:first + LANES])
            table = jnp.broadcast_to(table, index.shape)
            inside = (index >= first) & (index < first + LANES)
            value = jnp.take_along_axis(table, jnp.where(inside, index - first, 0), axis=1)
            found = jnp.where(inside, value, found)
        weight_ref[:, start:start + LANES] = found
    total = jnp.zeros((size, size), F32)
    for level in range(1, dist):
        total = total + qb_ref[level - 1] * row(size, -(dist - level) * size, -beta)
    branch_ref[...] = jnp.sum(total, axis=1, keepdims=True)


def main_kernel(dist, live_ref, qm_ref, *refs):
    rights = refs[:dist - 1]
    weight_ref, branch_ref, own_ref, end_ref, pair_ref, qm1_ref, out_ref = refs[dist - 1:]
    size = weight_ref.shape[0]
    beta = 1.0 / (dist * size)

    @pl.when(live_ref[0] == 0)
    def _():
        for ref in (pair_ref, qm1_ref, out_ref):
            ref[...] = jnp.zeros_like(ref)

    @pl.when(live_ref[0] != 0)
    def _():
        summed = jnp.zeros((size, size), F32)
        tail = jnp.zeros((1, size), F32)
        for shift in range(1, dist):
            right = rights[shift - 1][...]
            summed = summed + product(qm_ref[shift - 1], right)
            tail = tail + jnp.sum(right * column(size, shift * size, beta), axis=0, keepdims=True)
        rows = lax.broadcasted_iota(jnp.int32, (size, size), 0)
        columns = lax.broadcasted_iota(jnp.int32, (size, size), 1)
        upper = jnp.where(rows <= columns, 1.0, 0.0).astype(BF16)
        own = jnp.sum(jnp.where(rows == columns, own_ref[...], 0), axis=1, keepdims=True)
        both = own + end_ref[...]
        allowed = (both == 3) | (both == 5)
        pair = jnp.where(allowed, weight_ref[...] * (1.0 + 0.8 * summed), 0.0)
        pair_ref[...] = pair
        high, low = halves(pair * row(size, 0, -beta))
        branch = (branch_ref[...] + (dot(high, upper) + dot(low, upper))) * (row(size, 0, beta) * beta)
        qm1_ref[...] = branch
        high, low = halves(branch * column(size, 0, beta))
        start = tail + (dot(upper, high) + dot(upper, low))
        out_ref[...] = summed + start * (0.01 * column(size, 0, -beta))


def shifted(block, distance, width):
    return lax.ppermute(block, "row", [(i + distance, i) for i in range(width - distance)])


def per_device(qm, qm1, qb, codes, energy_index, turner):
    width = lax.axis_size("row")
    dist, size = qm.shape[2] + 1, qm.shape[3]
    live = (lax.axis_index("row") + dist < width).astype(jnp.int32).reshape(1)
    lives = width - dist
    rights = [
        lax.ppermute(qm1[0, 0, dist - shift - 1], "row", [(i + shift, i) for i in range(lives)])
        for shift in range(1, dist)
    ]
    own = codes[0]
    end = lax.ppermute(own, "row", [(i + dist, i) for i in range(lives)])
    vmem = pl.BlockSpec(memory_space=pltpu.VMEM)
    smem = pl.BlockSpec(memory_space=pltpu.SMEM)
    square = jax.ShapeDtypeStruct((size, size), F32)
    weight, branch = pl.pallas_call(
        functools.partial(weights_kernel, dist),
        out_shape=(square, jax.ShapeDtypeStruct((size, 1), F32)),
        in_specs=[vmem] * 3,
        out_specs=[vmem] * 2,
        compiler_params=pltpu.CompilerParams(vmem_limit_bytes=16 << 20),
        cost_estimate=pl.CostEstimate(flops=40 * size * size, bytes_accessed=4 * size * size * (dist + 1), transcendentals=0),
        name="weights",
    )(energy_index[0, 0], jnp.pad(turner, (0, -turner.shape[0] % LANES))[None], qb[0, 0])
    pair, branch, out = pl.pallas_call(
        functools.partial(main_kernel, dist),
        out_shape=(square,) * 3,
        in_specs=[smem] + [vmem] * (dist + 4),
        out_specs=[vmem] * 3,
        compiler_params=pltpu.CompilerParams(vmem_limit_bytes=32 << 20),
        name="blocks",
    )(live, qm[0, 0], *rights, weight, branch, own, end)
    return pair[None, None], branch[None, None], out[None, None]


def solution(mesh):
    blocks = P("seq", "row", None, None, None)
    return jax.shard_map(
        per_device,
        mesh=mesh,
        in_specs=(blocks, blocks, blocks, P("seq", "row", None), P("seq", "row", None, None), P()),
        out_specs=(P("seq", "row", None, None),) * 3,
        check_vma=False,
    )
```

time: 713 us -> 63.7 us (0.09)
  the two profiles are of different devices: /device:TPU:0 before, /device:TPU:6 now
where the time goes in v1:
time: 63.7 us; the launch traced here: 63.4 us
  waiting for transfers between devices  38.5 us (60%)
  starting transfers between devices  17.5 us (27%)
  Pallas kernels  3.93 us (6%)
  local copies, waits for them, and re-layouts  2.66 us (4%)
  between operations  0.8 us (1%)
    ppermute x7, waiting for transfers between devices, per_device(): lax.ppermute(qm1[0, 0, dist - shift - 1], 'row', [(i + shift, i) for i in...  25.2 us
    ppermute x7, starting transfers between devices, per_device(): lax.ppermute(qm1[0, 0, dist - shift - 1], 'row', [(i + shift, i) for i in...  16.2 us
    ppermute x1, waiting for transfers between devices, per_device(): end = lax.ppermute(own, 'row', [(i + dist, i) for i in range(lives)])  13.3 us
    pallas_call x1, Pallas kernels, per_device(): pl.pallas_call(functools.partial(main_kernel, dist), out_shape=(square,)...  3.6 us
    squeeze x1, local copies, waits for them, and re-layouts, per_device(): qm1[0, 0, dist - shift - 1]  2.64 us
    ppermute x1, starting transfers between devices, per_device(): end = lax.ppermute(own, 'row', [(i + dist, i) for i in range(lives)])  1.29 us
  transfers between devices with their start and end apart: 8, of which 4 were waited for; matrix products, arithmetic and copies ran while one was open for 0% of the time, Pallas kernels for 1%

profile of v1, /device:TPU:6, one launch (start us, length us, event | category | flops | bytes accessed | tf_op | source)
XLA Modules:
  0.0 63.4 jit_solution(12920620526492075661)
XLA Ops:
  0.6 0.0 copy-start.3
  0.6 0.0 copy-start.4
  0.7 0.0 copy-start.2
  0.7 0.0 copy-start
  0.7 2.6 %slice_bitcast_fusion = (f32[256,256]{1,0:T(8,128)S(1)}, f32[256,256]{1,0:T(8,128)S(1)}, f32[256,256]{1,0:T(8,128)}, f32[256,256]{1,0:T(8,128)}, f32[256,256]{1,...) fusion(f32[1,1,7,256,256]{4,3,2,1,0:T(8,128)} %param.7), kind=kLoop, calls=%fused_computation | loop fusion | bytes 3670016 | tf_op jit(solution)/shard_map/squeeze | solution.py:105
  3.3 1.3 %collective-permute-start.6 = (f32[256,256]{1,0:T(8,128)S(1)}, f32[256,256]{1,0:T(8,128)S(1)}, u32[]{:S(2)}, u32[]{:S(2)}) collective-permute-start(f32[256,256]{1,0:T(8,128)S(1)} %get-tuple-element.13), channel_id=1, source_target_pairs={{7,0},{8,1},{9,2},{10,3},{11,4},{12,5},{13,6},{14,7},{23,16},{24,1... | collective-permute-start | bytes 786440 | tf_op jit(solution)/shard_map/ppermute | solution.py:105
  4.6 1.3 %collective-permute-start.4 = (f32[256,256]{1,0:T(8,128)S(1)}, f32[256,256]{1,0:T(8,128)S(1)}, u32[]{:S(2)}, u32[]{:S(2)}) collective-permute-start(f32[256,256]{1,0:T(8,128)S(1)} %get-tuple-element.14), channel_id=1, source_target_pairs={{5,0},{6,1},{7,2},{8,3},{9,4},{10,5},{11,6},{12,7},{21,16},{22,17}... | collective-permute-start | bytes 786440 | tf_op jit(solution)/shard_map/ppermute | solution.py:105
  5.9 0.0 copy-done.3
  5.9 1.3 %collective-permute-start.7 = (s32[1,256]{1,0:T(1,128)S(1)}, s32[1,256]{1,0:T(1,128)S(1)}, u32[]{:S(2)}, u32[]{:S(2)}) collective-permute-start(s32[1,256]{1,0:T(1,128)S(1)} %bitcast.27), channel_id=1, source_target_pairs={{8,0},{9,1},{10,2},{11,3},{12,4},{13,5},{14,6},{15,7},{24,16},{25,... | collective-permute-start | bytes 3080 | tf_op jit(solution)/shard_map/ppermute | solution.py:109
  7.2 1.3 %collective-permute-start.3 = (f32[256,256]{1,0:T(8,128)}, f32[256,256]{1,0:T(8,128)S(1)}, u32[]{:S(2)}, u32[]{:S(2)}) collective-permute-start(f32[256,256]{1,0:T(8,128)} %get-tuple-element.15), channel_id=1, source_target_pairs={{4,0},{5,1},{6,2},{7,3},{8,4},{9,5},{10,6},{11,7},{20,16},{21,17},... | collective-permute-start | bytes 786440 | tf_op jit(solution)/shard_map/ppermute | solution.py:105
  8.5 1.3 %collective-permute-start.2 = (f32[256,256]{1,0:T(8,128)}, f32[256,256]{1,0:T(8,128)S(1)}, u32[]{:S(2)}, u32[]{:S(2)}) collective-permute-start(f32[256,256]{1,0:T(8,128)} %get-tuple-element.16), channel_id=1, source_target_pairs={{3,0},{4,1},{5,2},{6,3},{7,4},{8,5},{9,6},{10,7},{19,16},{20,17},{... | collective-permute-start | bytes 786440 | tf_op jit(solution)/shard_map/ppermute | solution.py:105
  9.8 13.3 %collective-permute-done.7.refs_10_ = s32[1,256]{1,0:T(1,128)S(1)} collective-permute-done((s32[1,256]{1,0:T(1,128)S(1)}, s32[1,256]{1,0:T(1,128)S(1)}, u32[]{:S(2)}, u32[]{:S(2)}) %collective-permute-start.7) | collective-permute-done | bytes 1056 | tf_op jit(solution)/shard_map/ppermute | solution.py:109
  23.1 7.2 %collective-permute-start.1 = (f32[256,256]{1,0:T(8,128)}, f32[256,256]{1,0:T(8,128)S(1)}, u32[]{:S(2)}, u32[]{:S(2)}) collective-permute-start(f32[256,256]{1,0:T(8,128)} %get-tuple-element.17), channel_id=1, source_target_pairs={{2,0},{3,1},{4,2},{5,3},{6,4},{7,5},{8,6},{9,7},{18,16},{19,17},{2... | collective-permute-start | bytes 786440 | tf_op jit(solution)/shard_map/ppermute | solution.py:105
  30.3 0.0 collective-permute-done.6.refs_6_
  30.3 2.6 %collective-permute-start = (f32[256,256]{1,0:T(8,128)}, f32[256,256]{1,0:T(8,128)}, u32[]{:S(2)}, u32[]{:S(2)}) collective-permute-start(f32[256,256]{1,0:T(8,128)} %get-tuple-element.18), channel_id=1, source_target_pairs={{1,0},{2,1},{3,2},{4,3},{5,4},{6,5},{7,6},{8,7},{17,16},{18,17},{1... | collective-permute-start | bytes 786440 | tf_op jit(solution)/shard_map/ppermute | solution.py:105
  32.9 0.0 collective-permute-done.4.refs_4_
  32.9 1.3 %collective-permute-start.5 = (f32[256,256]{1,0:T(8,128)}, f32[256,256]{1,0:T(8,128)}, u32[]{:S(2)}, u32[]{:S(2)}) collective-permute-start(f32[256,256]{1,0:T(8,128)} %get-tuple-element.19), channel_id=1, source_target_pairs={{6,0},{7,1},{8,2},{9,3},{10,4},{11,5},{12,6},{13,7},{22,16},{23,17... | collective-permute-start | bytes 786440 | tf_op jit(solution)/shard_map/ppermute | solution.py:105
  34.2 0.0 copy-done.4
  34.2 0.0 copy-start.1
  34.3 0.0 copy-done.2
  34.3 0.0 copy-done
  34.3 0.3 weights.1
  34.6 0.0 collective-permute-done.3.refs_3_
  34.6 0.0 collective-permute-done.2.refs_2_
  34.6 7.6 %collective-permute-done.1.refs_1_ = f32[256,256]{1,0:T(8,128)S(1)} collective-permute-done((f32[256,256]{1,0:T(8,128)}, f32[256,256]{1,0:T(8,128)S(1)}, u32[]{:S(2)}, u32[]{:S(2)}) %collective-permute-start.1) | collective-permute-done | bytes 262176 | tf_op jit(solution)/shard_map/ppermute | solution.py:105
  42.3 3.5 %collective-permute-done.refs_0_ = f32[256,256]{1,0:T(8,128)} collective-permute-done((f32[256,256]{1,0:T(8,128)}, f32[256,256]{1,0:T(8,128)}, u32[]{:S(2)}, u32[]{:S(2)}) %collective-permute-start) | collective-permute-done | bytes 262176 | tf_op jit(solution)/shard_map/ppermute | solution.py:105
  45.7 14.1 %collective-permute-done.5.refs_5_ = f32[256,256]{1,0:T(8,128)} collective-permute-done((f32[256,256]{1,0:T(8,128)}, f32[256,256]{1,0:T(8,128)}, u32[]{:S(2)}, u32[]{:S(2)}) %collective-permute-start.5) | collective-permute-done | bytes 262176 | tf_op jit(solution)/shard_map/ppermute | solution.py:105
  59.8 0.0 copy-done.1
  59.8 3.6 %blocks.1 = (f32[256,256]{1,0:T(8,128)}, f32[256,256]{1,0:T(8,128)}, f32[256,256]{1,0:T(8,128)}) custom-call(s32[1]{0:T(128)} %bitcast.live_ref, f32[7,256,256]{2,1,0:T(8,128)S(1)} %bitcast.25, f32[256,256]{1,0:T(8,128)} %collective-permute-done.refs_0_, f32[256,256]{1,0:T(8,128)S(1)} %collective-permute-done.1.refs_1_, ...), custom_call_target="tpu_custom_call" | custom-call | tf_op jit(solution)/shard_map/blocks/pallas_call | solution.py:122
  (1 shorter events, 0.0 us)
Async XLA Ops:
  0.6 5.3 %copy-start.3 = (s32[1,1,256]{2,1,0:T(1,128)S(1)}, s32[1,1,256]{2,1,0:T(1,128)}, u32[]{:S(2)}) copy-start(s32[1,1,256]{2,1,0:T(1,128)} %param.9) | copy-start | bytes 3076
  0.6 33.6 %copy-start.4 = (f32[64]{0:T(128)S(1)}, f32[64]{0:T(128)}, u32[]{:S(2)}) copy-start(f32[64]{0:T(128)} %param.11) | copy-start | bytes 772
  0.7 33.6 %copy-start.2 = (s32[1,1,256,256]{3,2,1,0:T(8,128)S(1)}, s32[1,1,256,256]{3,2,1,0:T(8,128)}, u32[]{:S(2)}) copy-start(s32[1,1,256,256]{3,2,1,0:T(8,128)} %param.10) | copy-start | bytes 786436
  0.7 33.6 %copy-start = (f32[1,1,7,256,256]{4,3,2,1,0:T(8,128)S(1)}, f32[1,1,7,256,256]{4,3,2,1,0:T(8,128)}, u32[]{:S(2)}) copy-start(f32[1,1,7,256,256]{4,3,2,1,0:T(8,128)} %param.8) | copy-start | bytes 5505028
  3.3 27.0 %collective-permute-start.6 = (f32[256,256]{1,0:T(8,128)S(1)}, f32[256,256]{1,0:T(8,128)S(1)}, u32[]{:S(2)}, u32[]{:S(2)}) collective-permute-start(f32[256,256]{1,0:T(8,128)S(1)} %get-tuple-element.13), channel_id=1, source_target_pairs={{7,0},{8,1},{9,2},{10,3},{11,4},{12,5},{13,6},{14,7},{23,16},{24,1... | collective-permute-start | bytes 786440 | tf_op jit(solution)/shard_map/ppermute | solution.py:105
  4.6 28.3 %collective-permute-start.4 = (f32[256,256]{1,0:T(8,128)S(1)}, f32[256,256]{1,0:T(8,128)S(1)}, u32[]{:S(2)}, u32[]{:S(2)}) collective-permute-start(f32[256,256]{1,0:T(8,128)S(1)} %get-tuple-element.14), channel_id=1, source_target_pairs={{5,0},{6,1},{7,2},{8,3},{9,4},{10,5},{11,6},{12,7},{21,16},{22,17}... | collective-permute-start | bytes 786440 | tf_op jit(solution)/shard_map/ppermute | solution.py:105
  5.9 17.2 %collective-permute-start.7 = (s32[1,256]{1,0:T(1,128)S(1)}, s32[1,256]{1,0:T(1,128)S(1)}, u32[]{:S(2)}, u32[]{:S(2)}) collective-permute-start(s32[1,256]{1,0:T(1,128)S(1)} %bitcast.27), channel_id=1, source_target_pairs={{8,0},{9,1},{10,2},{11,3},{12,4},{13,5},{14,6},{15,7},{24,16},{25,... | collective-permute-start | bytes 3080 | tf_op jit(solution)/shard_map/ppermute | solution.py:109
  7.2 27.4 %collective-permute-start.3 = (f32[256,256]{1,0:T(8,128)}, f32[256,256]{1,0:T(8,128)S(1)}, u32[]{:S(2)}, u32[]{:S(2)}) collective-permute-start(f32[256,256]{1,0:T(8,128)} %get-tuple-element.15), channel_id=1, source_target_pairs={{4,0},{5,1},{6,2},{7,3},{8,4},{9,5},{10,6},{11,7},{20,16},{21,17},... | collective-permute-start | bytes 786440 | tf_op jit(solution)/shard_map/ppermute | solution.py:105
  8.5 26.1 %collective-permute-start.2 = (f32[256,256]{1,0:T(8,128)}, f32[256,256]{1,0:T(8,128)S(1)}, u32[]{:S(2)}, u32[]{:S(2)}) collective-permute-start(f32[256,256]{1,0:T(8,128)} %get-tuple-element.16), channel_id=1, source_target_pairs={{3,0},{4,1},{5,2},{6,3},{7,4},{8,5},{9,6},{10,7},{19,16},{20,17},{... | collective-permute-start | bytes 786440 | tf_op jit(solution)/shard_map/ppermute | solution.py:105
  23.1 19.1 %collective-permute-start.1 = (f32[256,256]{1,0:T(8,128)}, f32[256,256]{1,0:T(8,128)S(1)}, u32[]{:S(2)}, u32[]{:S(2)}) collective-permute-start(f32[256,256]{1,0:T(8,128)} %get-tuple-element.17), channel_id=1, source_target_pairs={{2,0},{3,1},{4,2},{5,3},{6,4},{7,5},{8,6},{9,7},{18,16},{19,17},{2... | collective-permute-start | bytes 786440 | tf_op jit(solution)/shard_map/ppermute | solution.py:105
  30.3 15.4 %collective-permute-start = (f32[256,256]{1,0:T(8,128)}, f32[256,256]{1,0:T(8,128)}, u32[]{:S(2)}, u32[]{:S(2)}) collective-permute-start(f32[256,256]{1,0:T(8,128)} %get-tuple-element.18), channel_id=1, source_target_pairs={{1,0},{2,1},{3,2},{4,3},{5,4},{6,5},{7,6},{8,7},{17,16},{18,17},{1... | collective-permute-start | bytes 786440 | tf_op jit(solution)/shard_map/ppermute | solution.py:105
  32.9 26.9 %collective-permute-start.5 = (f32[256,256]{1,0:T(8,128)}, f32[256,256]{1,0:T(8,128)}, u32[]{:S(2)}, u32[]{:S(2)}) collective-permute-start(f32[256,256]{1,0:T(8,128)} %get-tuple-element.19), channel_id=1, source_target_pairs={{6,0},{7,1},{8,2},{9,3},{10,4},{11,5},{12,6},{13,7},{22,16},{23,17... | collective-permute-start | bytes 786440 | tf_op jit(solution)/shard_map/ppermute | solution.py:105
  34.2 25.6 %copy-start.1 = (f32[1,1,7,256,256]{4,3,2,1,0:T(8,128)S(1)}, f32[1,1,7,256,256]{4,3,2,1,0:T(8,128)}, u32[]{:S(2)}) copy-start(f32[1,1,7,256,256]{4,3,2,1,0:T(8,128)} %param.6) | copy-start | bytes 5505028

commit v2 on v1

--- a/solution.py
+++ b/solution.py
@@ -2,6 +2,7 @@
 
 import jax
 import jax.numpy as jnp
+import numpy as np
 from jax import lax
 from jax.experimental import pallas as pl
 from jax.experimental.pallas import tpu as pltpu
@@ -10,6 +11,98 @@
 F32 = jnp.float32
 BF16 = jnp.bfloat16
 LANES = 128
+FIRST = 1
+LATE = 4
+GATE = 1
+PLAN = (
+    (5, (5, 6, 7), (0, 4, 2, 3, -1, 1, 0)),
+    (3, (3, 4, 5), (1, 4, -1, 1, 0, 2, 3)),
+    (5, (5, 6, 7), (0, 2, 4, 3, -1, 1, 0)),
+    (3, (3, 4, 5), (4, 2, -1, 1, 0, 3, 1)),
+    (4, (4, 5, 7), (1, 0, 3, -1, 2, 4, 0)),
+    (4, (3, 4, 7), (1, 0, 2, -1, 3, 4, 0)),
+    (5, (3, 6, 7), (1, 0, 1, 2, 3, 2, 0)),
+    (3, (3, 4, 6), (1, 0, -1, 1, 4, 2, 2)),
+)
+
+
+def colored(flows):
+    count = max(max(np.bincount([f[end] for f in flows])) for end in (0, 1))
+    used = {}
+    rounds = []
+    for number, (source, target) in enumerate(flows):
+        free = [[c for c in range(count) if (end, at, c) not in used] for end, at in ((0, source), (1, target))]
+        common = [c for c in free[0] if c in free[1]]
+        rounds.append(common[0] if common else free[0][0])
+        if not common:
+            first, second = free[0][0], free[1][0]
+            chain, end, at, want = [], 1, target, first
+            while (end, at, want) in used:
+                other = used[end, at, want]
+                chain.append(other)
+                end, at = 1 - end, flows[other][1 - end]
+                want = first + second - want
+            for other in chain:
+                for side in (0, 1):
+                    del used[side, flows[other][side], rounds[other]]
+            for other in chain:
+                rounds[other] = first + second - rounds[other]
+                for side in (0, 1):
+                    used[side, flows[other][side], rounds[other]] = other
+        for side in (0, 1):
+            used[side, flows[number][side], rounds[number]] = number
+    return rounds, count
+
+
+class Plan:
+    def __init__(self, width, dist):
+        self.lives = lives = max(width - dist, 0)
+        far = {}
+        routes = {}
+        for i in range(lives):
+            offset, products, hints = PLAN[i % len(PLAN)]
+            if i + offset < width and max(products) < dist:
+                far[i] = (i + offset, products)
+            for m in range(1, dist):
+                at = far[i][0] if i in far and m in far[i][1] else i
+                if at != i + m:
+                    routes.setdefault((i + m, at), []).append((at == i, i, m, hints[m - 1] if m <= len(hints) else -1))
+        rounds = {route: blocks[0][3] for route, blocks in routes.items()}
+        ends = [(side, route[side], t) for route, t in rounds.items() for side in (0, 1)]
+        if len(set(ends)) < len(ends) or min(rounds.values(), default=0) < 0:
+            order = sorted(routes, key=lambda route: -len(routes[route]))
+            rounds = dict(zip(order, colored(order)[0]))
+        self.rounds = max(rounds.values(), default=-1) + 1
+        self.pairs = [[route for route in routes if rounds[route] == t] for t in range(self.rounds)]
+        self.sizes = [max(len(routes[route]) for route in pairs) for pairs in self.pairs]
+        self.slots = slots = max([len(products) for _, products in far.values()], default=0)
+        starts = np.concatenate([[0], np.cumsum(self.sizes)]).astype(int)
+        self.send = np.full((starts[-1], width), -1, np.int32)
+        self.near = np.full((starts[-1], width), -1, np.int32)
+        far_slot = np.full((starts[-1], width), -1, np.int32)
+        for (source, target), blocks in routes.items():
+            for line, (is_near, i, m, _) in enumerate(sorted(blocks), starts[rounds[source, target]]):
+                self.send[line, source] = dist - 1 - m
+                if is_near:
+                    self.near[line, target] = m
+                else:
+                    far_slot[line, target] = far[i][1].index(m)
+        self.starts = starts
+        self.places = [(t, at) for t, count in enumerate(self.sizes) for at in range(count)]
+        lines = [line for line in range(starts[-1]) if far_slot[line].max() >= 0]
+        self.far_rounds = sorted({self.places[line][0] for line in lines})
+        self.far_places = [(self.far_rounds.index(t), at) for t, at in (self.places[line] for line in lines)]
+        self.moved = np.full((slots, width), -1, np.int32)
+        far_m = np.full((slots, width), -1, np.int32)
+        own = np.full((1, width), -1, np.int32)
+        for i, (at, products) in far.items():
+            self.moved[:len(products), i] = np.array(products) - 1
+            far_m[:len(products), at] = products
+            if at - i in products:
+                own[0, at] = products.index(at - i)
+        self.far = np.concatenate([far_m, far_slot[lines], own])
+        self.there = [(i, at) for i, (at, _) in far.items()]
+        self.back = [(at, i) for i, at in self.there]
 
 
 def halves(x):
@@ -57,25 +150,84 @@
     branch_ref[...] = jnp.sum(total, axis=1, keepdims=True)
 
 
-def main_kernel(dist, live_ref, qm_ref, *refs):
-    rights = refs[:dist - 1]
-    weight_ref, branch_ref, own_ref, end_ref, pair_ref, qm1_ref, out_ref = refs[dist - 1:]
+def looked_up(table, me):
+    entries = []
+    for first in range(0, len(table), 7):
+        lines = table[first:first + 7].astype(np.int64) + 1
+        words = sum(line << (4 * at) for at, line in enumerate(lines))
+        word = jnp.int32(0)
+        for column, value in enumerate(words):
+            word = jnp.where(me == column, jnp.int32(value), word)
+        entries += [((word >> (4 * at)) & 15) - 1 for at in range(len(lines))]
+    return entries
+
+
+def pick_kernel(tables, *refs):
+    me = lax.axis_index("row")
+    sems = refs[-1]
+    operands, places = refs[:len(tables)], refs[len(tables):-1]
+    places = [ref.at[slot] for ref in places for slot in range(ref.shape[0])]
+    copies = []
+    for table, operand in zip(tables, operands):
+        for entry in looked_up(table, me):
+            number = len(copies)
+            copy = pltpu.make_async_copy(operand.at[jnp.maximum(entry, 0)], places[number], sems.at[number])
+            copies.append((entry >= 0, copy))
+    for wanted, copy in copies:
+        pl.when(wanted)(copy.start)
+    for wanted, copy in copies:
+        pl.when(wanted)(copy.wait)
+
+
+def far_kernel(plan, dist, table_ref, qm1_ref, left_ref, *refs):
+    me = lax.axis_index("row")
+    rights, out_ref = refs[:-1], refs[-1]
+    size = out_ref.shape[1]
+    beta = 1.0 / (dist * size)
+    out_ref[...] = jnp.zeros_like(out_ref)
+    blocks = [rights[t].at[at] for t, at in plan.far_places]
+    for number, right_ref in enumerate(blocks + [None]):
+        slot = table_ref[plan.slots + number, me]
+
+        @pl.when(slot >= 0)
+        def _():
+            m = table_ref[jnp.maximum(slot, 0), me]
+            right = right_ref[...] if right_ref is not None else qm1_ref[dist - 1 - m]
+            out_ref[:size] += product(left_ref[jnp.maximum(slot, 0)], right)
+            out_ref[size:size + 1] += jnp.sum(right * column(size, m * size, beta), axis=0, keepdims=True)
+
+
+def near_kernel(plan, dist, table_ref, qm_ref, *refs):
+    me = lax.axis_index("row")
+    rights, out_ref = refs[:-1], refs[-1]
+    size = out_ref.shape[1]
+    beta = 1.0 / (dist * size)
+    out_ref[...] = jnp.zeros_like(out_ref)
+    for number, (t, at) in enumerate(plan.places):
+        right_ref = rights[t].at[at]
+        m = table_ref[number, me]
+
+        @pl.when(m >= 0)
+        def _():
+            right = right_ref[...]
+            out_ref[:size] += product(qm_ref[m - 1], right)
+            out_ref[size:size + 1] += jnp.sum(right * column(size, m * size, beta), axis=0, keepdims=True)
+
+
+def last_kernel(plan, dist, near_ref, far_ref, weight_ref, branch_ref, own_ref, end_ref, pair_ref, qm1_ref, out_ref):
+    live = lax.axis_index("row") < plan.lives
     size = weight_ref.shape[0]
     beta = 1.0 / (dist * size)
 
-    @pl.when(live_ref[0] == 0)
+    @pl.when(jnp.logical_not(live))
     def _():
         for ref in (pair_ref, qm1_ref, out_ref):
             ref[...] = jnp.zeros_like(ref)
 
-    @pl.when(live_ref[0] != 0)
+    @pl.when(live)
     def _():
-        summed = jnp.zeros((size, size), F32)
-        tail = jnp.zeros((1, size), F32)
-        for shift in range(1, dist):
-            right = rights[shift - 1][...]
-            summed = summed + product(qm_ref[shift - 1], right)
-            tail = tail + jnp.sum(right * column(size, shift * size, beta), axis=0, keepdims=True)
+        summed = near_ref[:size] + far_ref[:size]
+        tail = near_ref[size:size + 1] + far_ref[size:size + 1]
         rows = lax.broadcasted_iota(jnp.int32, (size, size), 0)
         columns = lax.broadcasted_iota(jnp.int32, (size, size), 1)
         upper = jnp.where(rows <= columns, 1.0, 0.0).astype(BF16)
@@ -92,41 +244,75 @@
         out_ref[...] = summed + start * (0.01 * column(size, 0, -beta))
 
 
-def shifted(block, distance, width):
-    return lax.ppermute(block, "row", [(i + distance, i) for i in range(width - distance)])
-
-
 def per_device(qm, qm1, qb, codes, energy_index, turner):
     width = lax.axis_size("row")
     dist, size = qm.shape[2] + 1, qm.shape[3]
-    live = (lax.axis_index("row") + dist < width).astype(jnp.int32).reshape(1)
-    lives = width - dist
-    rights = [
-        lax.ppermute(qm1[0, 0, dist - shift - 1], "row", [(i + shift, i) for i in range(lives)])
-        for shift in range(1, dist)
-    ]
-    own = codes[0]
-    end = lax.ppermute(own, "row", [(i + dist, i) for i in range(lives)])
+    plan = Plan(width, dist)
+    qm, qm1, qb, index = qm[0, 0], qm1[0, 0], qb[0, 0], energy_index[0, 0]
     vmem = pl.BlockSpec(memory_space=pltpu.VMEM)
     smem = pl.BlockSpec(memory_space=pltpu.SMEM)
+    hbm = pl.BlockSpec(memory_space=pltpu.HBM)
     square = jax.ShapeDtypeStruct((size, size), F32)
-    weight, branch = pl.pallas_call(
-        functools.partial(weights_kernel, dist),
-        out_shape=(square, jax.ShapeDtypeStruct((size, 1), F32)),
-        in_specs=[vmem] * 3,
-        out_specs=[vmem] * 2,
-        compiler_params=pltpu.CompilerParams(vmem_limit_bytes=16 << 20),
-        cost_estimate=pl.CostEstimate(flops=40 * size * size, bytes_accessed=4 * size * size * (dist + 1), transcendentals=0),
-        name="weights",
-    )(energy_index[0, 0], jnp.pad(turner, (0, -turner.shape[0] % LANES))[None], qb[0, 0])
-    pair, branch, out = pl.pallas_call(
-        functools.partial(main_kernel, dist),
-        out_shape=(square,) * 3,
-        in_specs=[smem] + [vmem] * (dist + 4),
-        out_specs=[vmem] * 3,
-        compiler_params=pltpu.CompilerParams(vmem_limit_bytes=32 << 20),
-        name="blocks",
-    )(live, qm[0, 0], *rights, weight, branch, own, end)
+    tall = jax.ShapeDtypeStruct((size + 8, size), F32)
+
+    def call(kernel, name, outs, ins, args, products, scratch=(), vmem_mib=40):
+        many = isinstance(outs, tuple)
+        return pl.pallas_call(
+            kernel,
+            out_shape=outs,
+            in_specs=ins,
+            out_specs=(vmem,) * len(outs) if many else vmem,
+            scratch_shapes=scratch,
+            compiler_params=pltpu.CompilerParams(vmem_limit_bytes=vmem_mib << 20),
+            cost_estimate=pl.CostEstimate(
+                flops=products * 6 * size**3, bytes_accessed=4 * size * size * (dist + 1), transcendentals=0
+            ),
+            name=name,
+        )(*args)
+
+    rounds = plan.rounds
+    first = min(FIRST, rounds)
+    stack = [jax.ShapeDtypeStruct((count, size, size), F32) for count in [plan.slots] + plan.sizes]
+    cut = plan.starts[first]
+
+    def pick(name, operands, tables, outs):
+        lines = sum(len(table) for table in tables)
+        return call(
+            functools.partial(pick_kernel, tables), name, outs, [hbm] * len(operands), operands, 0,
+            [pltpu.SemaphoreType.DMA((lines,))], 60,
+        )
+
+    picked = pick("pick_first", (qm, qm1), (plan.moved, plan.send[:cut]), tuple(stack[:first + 1]))
+    left, blocks = picked[0], picked[1:]
+    blocks += pick("pick_rest", (qm1,), (plan.send[cut:],), tuple(stack[first + 1:]))
+    left = lax.ppermute(left, "row", plan.there)
+    early = [t for t in range(rounds) if t < LATE or t in plan.far_rounds]
+    late = [t for t in range(rounds) if t not in early]
+    rights = {t: lax.ppermute(blocks[t], "row", plan.pairs[t]) for t in early}
+    own = codes[0]
+    end = lax.ppermute(own, "row", [(i + dist, i) for i in range(plan.lives)])
+    weight, branch = call(
+        functools.partial(weights_kernel, dist), "weights", (square, jax.ShapeDtypeStruct((size, 1), F32)), [vmem] * 3,
+        (index, jnp.pad(turner, (0, -turner.shape[0] % LANES))[None], qb), 0,
+    )
+    far = call(
+        functools.partial(far_kernel, plan, dist), "far", tall, [smem] + [vmem] * (2 + len(plan.far_rounds)),
+        (jnp.asarray(plan.far), qm1, left, *(rights[t] for t in plan.far_rounds)), 3,
+    )
+    if late and GATE:
+        held, far = lax.optimization_barrier(([blocks[t] for t in late], far))
+    else:
+        held = [blocks[t] for t in late]
+    far = lax.ppermute(far, "row", plan.back)
+    rights.update((t, lax.ppermute(block, "row", plan.pairs[t])) for t, block in zip(late, held))
+    near = call(
+        functools.partial(near_kernel, plan, dist), "near", tall, [smem] + [vmem] * (1 + rounds),
+        (jnp.asarray(plan.near), qm, *(rights[t] for t in range(rounds))), 7,
+    )
+    pair, branch, out = call(
+        functools.partial(last_kernel, plan, dist), "last", (square,) * 3, [vmem] * 6,
+        (near, far, weight, branch, own, end), 2,
+    )
     return pair[None, None], branch[None, None], out[None, None]
 
 

time: 63.7 us -> 49.4 us (0.78)
  the two profiles are of different devices: /device:TPU:6 before, /device:TPU:0 now
where the time goes in v2:
time: 49.4 us; the launch traced here: 49.1 us
  waiting for transfers between devices  27.2 us (55%)
  starting transfers between devices  13.3 us (27%)
  Pallas kernels  7.78 us (16%)
  between operations  0.85 us (2%)
    ppermute x4, waiting for transfers between devices, per_device(): rights = {t: lax.ppermute(blocks[t], 'row', plan.pairs[t]) for t in early}  11 us
    ppermute x1, waiting for transfers between devices, per_device(): end = lax.ppermute(own, 'row', [(i + dist, i) for i in range(plan.lives)])  8.79 us
    pallas_call x6, Pallas kernels, call(): pl.pallas_call(kernel, out_shape=outs, in_specs=ins, out_specs=(vmem,) *...  7.78 us
    ppermute x4, starting transfers between devices, per_device(): rights = {t: lax.ppermute(blocks[t], 'row', plan.pairs[t]) for t in early}  4.7 us
    ppermute x1, starting transfers between devices, per_device(): left = lax.ppermute(left, 'row', plan.there)  4.55 us
    ppermute x1, waiting for transfers between devices, per_device(): lax.ppermute(block, 'row', plan.pairs[t])  3.98 us
    ppermute x1, waiting for transfers between devices, per_device(): far = lax.ppermute(far, 'row', plan.back)  2.16 us
    ppermute x1, starting transfers between devices, per_device(): lax.ppermute(block, 'row', plan.pairs[t])  1.42 us
  transfers between devices with their start and end apart: 8, of which 5 were waited for; matrix products, arithmetic and copies ran while one was open for 0% of the time, Pallas kernels for 8%

profile of v2, /device:TPU:0, one launch (start us, length us, event | category | flops | bytes accessed | tf_op | source)
XLA Modules:
  0.0 49.1 jit_solution(10636226469792516415)
XLA Ops:
  0.6 2.3 %pick_first.1 = (f32[3,256,256]{2,1,0:T(8,128)}, f32[2,256,256]{2,1,0:T(8,128)}) custom-call(f32[7,256,256]{2,1,0:T(8,128)} %bitcast.13, f32[7,256,256]{2,1,0:T(8,128)} %bitcast.10), custom_call_target="tpu_custom_call" | custom-call | bytes 2359296 | tf_op jit(solution)/shard_map/pick_first/pallas_call | solution.py:260
  2.9 0.0 copy-start
  2.9 0.0 copy-start.5
  2.9 4.5 %collective-permute-start.4 = (f32[3,256,256]{2,1,0:T(8,128)}, f32[3,256,256]{2,1,0:T(8,128)S(1)}, u32[]{:S(2)}, u32[]{:S(2)}) collective-permute-start(f32[3,256,256]{2,1,0:T(8,128)} %get-tuple-element.21), channel_id=1, source_target_pairs={{0,5},{1,4},{2,7},{3,6},{4,8},{5,9},{6,11},{7,10},{16,21},{17,20},... | collective-permute-start | bytes 2359304 | tf_op jit(solution)/shard_map/ppermute | solution.py:288
  7.5 1.3 %collective-permute-start = (f32[2,256,256]{2,1,0:T(8,128)}, f32[2,256,256]{2,1,0:T(8,128)S(1)}, u32[]{:S(2)}, u32[]{:S(2)}) collective-permute-start(f32[2,256,256]{2,1,0:T(8,128)} %get-tuple-element.16), channel_id=1, source_target_pairs={{1,0},{7,5},{6,4},{3,2},{9,7},{8,6},{11,8},{12,9},{13,11},{17,16},... | collective-permute-start | bytes 1572872 | tf_op jit(solution)/shard_map/ppermute | solution.py:291
  8.8 1.1 %pick_rest.1 = (f32[2,256,256]{2,1,0:T(8,128)}, f32[1,256,256]{2,1,0:T(8,128)}, f32[1,256,256]{2,1,0:T(8,128)}, f32[1,256,256]{2,1,0:T(8,128)}) custom-call(f32[7,256,256]{2,1,0:T(8,128)} %bitcast.11), custom_call_target="tpu_custom_call" | custom-call | bytes 2359296 | tf_op jit(solution)/shard_map/pick_rest/pallas_call | solution.py:260
  9.9 0.7 %collective-permute-start.1 = (f32[2,256,256]{2,1,0:T(8,128)}, f32[2,256,256]{2,1,0:T(8,128)S(1)}, u32[]{:S(2)}, u32[]{:S(2)}) collective-permute-start(f32[2,256,256]{2,1,0:T(8,128)} %get-tuple-element.17), channel_id=1, source_target_pairs={{6,5},{2,1},{5,4},{8,7},{7,6},{10,3},{9,11},{11,10},{22,21},{18,17... | collective-permute-start | bytes 1572872 | tf_op jit(solution)/shard_map/ppermute | solution.py:291
  10.6 1.3 %collective-permute-start.2 = (f32[1,256,256]{2,1,0:T(8,128)}, f32[1,256,256]{2,1,0:T(8,128)S(1)}, u32[]{:S(2)}, u32[]{:S(2)}) collective-permute-start(f32[1,256,256]{2,1,0:T(8,128)} %get-tuple-element.18), channel_id=1, source_target_pairs={{3,0},{7,1},{4,2},{5,3},{9,8},{8,9},{10,6},{12,11},{13,10},{14,7},... | collective-permute-start | bytes 786440 | tf_op jit(solution)/shard_map/ppermute | solution.py:291
  11.9 0.0 copy-start.7
  11.9 0.0 copy-start.6
  11.9 0.0 copy-start.8
  12.0 0.0 copy-start.2
  12.0 0.0 copy-start.3
  12.0 1.4 %collective-permute-start.3 = (f32[1,256,256]{2,1,0:T(8,128)}, f32[1,256,256]{2,1,0:T(8,128)S(1)}, u32[]{:S(2)}, u32[]{:S(2)}) collective-permute-start(f32[1,256,256]{2,1,0:T(8,128)} %get-tuple-element.19), channel_id=1, source_target_pairs={{4,0},{8,1},{6,2},{9,3},{7,4},{10,5},{11,6},{20,16},{24,17},{22,18... | collective-permute-start | bytes 786440 | tf_op jit(solution)/shard_map/ppermute | solution.py:291
  13.4 11.0 %collective-permute-done.2.refs_2_ = f32[1,256,256]{2,1,0:T(8,128)S(1)} collective-permute-done((f32[1,256,256]{2,1,0:T(8,128)}, f32[1,256,256]{2,1,0:T(8,128)S(1)}, u32[]{:S(2)}, u32[]{:S(2)}) %collective-permute-start.2) | collective-permute-done | bytes 262176 | tf_op jit(solution)/shard_map/ppermute | solution.py:291
  24.4 0.0 collective-permute-done.refs_0_
  24.4 0.0 collective-permute-done.1.refs_1_
  24.4 1.3 %collective-permute-done.4.left_ref = f32[3,256,256]{2,1,0:T(8,128)S(1)} collective-permute-done((f32[3,256,256]{2,1,0:T(8,128)}, f32[3,256,256]{2,1,0:T(8,128)S(1)}, u32[]{:S(2)}, u32[]{:S(2)}) %collective-permute-start.4) | collective-permute-done | bytes 786464 | tf_op jit(solution)/shard_map/ppermute | solution.py:288
  25.6 0.0 copy-done
  25.6 0.0 copy-done.5
  25.7 0.6 %far.1 = f32[264,256]{1,0:T(8,128)S(1)} custom-call(s32[7,16]{1,0:T(8,128)S(1)} %copy-done.5, f32[7,256,256]{2,1,0:T(8,128)S(1)} %bitcast.12, f32[3,256,256]{2,1,0:T(8,128)S(1)} %collective-permute-done.4.left_ref, f32[2,256,256]{2,1,0:T(8,128)S(1)} %collective-permute-done.refs_0_, f32[2,256,256]{2,1,0:T(8,128)S(1)} %collective-permute-done.1.refs_1_, ...), custom_call_target="tpu_custom_call" | custom-call | flops 301989888 | bytes 2359296 | tf_op jit(solution)/shard_map/far/pallas_call | solution.py:260
  26.3 0.0 copy-start.1
  26.3 0.0 copy-start.4
  26.3 0.0 copy-done.7
  26.3 1.4 %collective-permute-start.5 = (f32[1,256,256]{2,1,0:T(8,128)S(1)}, f32[1,256,256]{2,1,0:T(8,128)S(1)}, u32[]{:S(2)}, u32[]{:S(2)}) collective-permute-start(f32[1,256,256]{2,1,0:T(8,128)S(1)} %copy-done.7), channel_id=1, source_target_pairs={{2,0},{3,1},{5,2},{4,3},{10,4},{11,5},{12,7},{18,16},{19,17},{21,1... | collective-permute-start | bytes 786440 | tf_op jit(solution)/shard_map/ppermute | solution.py:307
  27.8 1.3 %collective-permute-start.6 = (f32[264,256]{1,0:T(8,128)S(1)}, f32[264,256]{1,0:T(8,128)S(1)}, u32[]{:S(2)}, u32[]{:S(2)}) collective-permute-start(f32[264,256]{1,0:T(8,128)S(1)} %far.1), channel_id=1, source_target_pairs={{5,0},{4,1},{7,2},{6,3},{8,4},{9,5},{11,6},{10,7},{21,16},{20,17},... | collective-permute-start | bytes 811016 | tf_op jit(solution)/shard_map/ppermute | solution.py:306
  29.1 0.0 copy-done.6
  29.1 1.3 %collective-permute-start.7 = (s32[1,256]{1,0:T(1,128)S(1)}, s32[1,256]{1,0:T(1,128)S(1)}, u32[]{:S(2)}, u32[]{:S(2)}) collective-permute-start(s32[1,256]{1,0:T(1,128)S(1)} %bitcast.17), channel_id=1, source_target_pairs={{8,0},{9,1},{10,2},{11,3},{12,4},{13,5},{14,6},{15,7},{24,16},{25,... | collective-permute-start | bytes 3080 | tf_op jit(solution)/shard_map/ppermute | solution.py:293
  30.4 0.0 copy-done.8
  30.4 0.0 copy-done.2
  30.4 0.0 copy-done.3
  30.4 0.3 weights.1
  30.8 0.0 collective-permute-done.3.refs_3_
  30.8 4.0 %collective-permute-done.5.refs_4_ = f32[1,256,256]{2,1,0:T(8,128)S(1)} collective-permute-done((f32[1,256,256]{2,1,0:T(8,128)S(1)}, f32[1,256,256]{2,1,0:T(8,128)S(1)}, u32[]{:S(2)}, u32[]{:S(2)}) %collective-permute-start.5) | collective-permute-done | bytes 262176 | tf_op jit(solution)/shard_map/ppermute | solution.py:307
  34.7 0.0 copy-done.1
  34.7 0.0 copy-done.4
  34.7 1.9 %near.1.near_ref = f32[264,256]{1,0:T(8,128)S(1)} custom-call(s32[7,16]{1,0:T(8,128)S(1)} %copy-done.4, f32[7,256,256]{2,1,0:T(8,128)S(1)} %bitcast.14, f32[2,256,256]{2,1,0:T(8,128)S(1)} %collective-permute-done.refs_0_, f32[2,256,256]{2,1,0:T(8,128)S(1)} %collective-permute-done.1.refs_1_, f32[1,256,256]{2,1,0:T(8,128)S(1)} %collective-permute-done.2.refs_2_, ...), custom_call_target="tpu_custom_call" | custom-call | flops 704643072 | bytes 2359296 | tf_op jit(solution)/shard_map/near/pallas_call | solution.py:260
  36.6 8.8 %collective-permute-done.7.end_ref = s32[1,256]{1,0:T(1,128)S(1)} collective-permute-done((s32[1,256]{1,0:T(1,128)S(1)}, s32[1,256]{1,0:T(1,128)S(1)}, u32[]{:S(2)}, u32[]{:S(2)}) %collective-permute-start.7) | collective-permute-done | bytes 1056 | tf_op jit(solution)/shard_map/ppermute | solution.py:293
  45.4 2.2 %collective-permute-done.6.far_ref = f32[264,256]{1,0:T(8,128)S(1)} collective-permute-done((f32[264,256]{1,0:T(8,128)S(1)}, f32[264,256]{1,0:T(8,128)S(1)}, u32[]{:S(2)}, u32[]{:S(2)}) %collective-permute-start.6) | collective-permute-done | bytes 270368 | tf_op jit(solution)/shard_map/ppermute | solution.py:306
  47.6 1.5 %last.1 = (f32[256,256]{1,0:T(8,128)}, f32[256,256]{1,0:T(8,128)}, f32[256,256]{1,0:T(8,128)}) custom-call(f32[264,256]{1,0:T(8,128)S(1)} %near.1.near_ref, f32[264,256]{1,0:T(8,128)S(1)} %collective-permute-done.6.far_ref, f32[256,256]{1,0:T(8,128)S(1)} %get-tuple-element.24.weight_ref, f32[256,1]{1,0:T(8,128)S(1)} %get-tuple-element.25.branch_ref, ...), custom_call_target="tpu_custom_call" | custom-call | flops 201326592 | bytes 2359296 | tf_op jit(solution)/shard_map/last/pallas_call | solution.py:260
  (1 shorter events, 0.0 us)
Async XLA Ops:
  2.9 22.8 %copy-start = (f32[1,1,7,256,256]{4,3,2,1,0:T(8,128)S(1)}, f32[1,1,7,256,256]{4,3,2,1,0:T(8,128)}, u32[]{:S(2)}) copy-start(f32[1,1,7,256,256]{4,3,2,1,0:T(8,128)} %param.9) | copy-start | bytes 5505028
  2.9 22.7 %copy-start.5 = (s32[7,16]{1,0:T(8,128)S(1)}, s32[7,16]{1,0:T(8,128)}, u32[]{:S(2)}) copy-start(s32[7,16]{1,0:T(8,128)} %constant.7.clone.table_ref) | copy-start | bytes 1348
  2.9 22.7 %collective-permute-start.4 = (f32[3,256,256]{2,1,0:T(8,128)}, f32[3,256,256]{2,1,0:T(8,128)S(1)}, u32[]{:S(2)}, u32[]{:S(2)}) collective-permute-start(f32[3,256,256]{2,1,0:T(8,128)} %get-tuple-element.21), channel_id=1, source_target_pairs={{0,5},{1,4},{2,7},{3,6},{4,8},{5,9},{6,11},{7,10},{16,21},{17,20},... | collective-permute-start | bytes 2359304 | tf_op jit(solution)/shard_map/ppermute | solution.py:288
  7.5 16.9 %collective-permute-start = (f32[2,256,256]{2,1,0:T(8,128)}, f32[2,256,256]{2,1,0:T(8,128)S(1)}, u32[]{:S(2)}, u32[]{:S(2)}) collective-permute-start(f32[2,256,256]{2,1,0:T(8,128)} %get-tuple-element.16), channel_id=1, source_target_pairs={{1,0},{7,5},{6,4},{3,2},{9,7},{8,6},{11,8},{12,9},{13,11},{17,16},... | collective-permute-start | bytes 1572872 | tf_op jit(solution)/shard_map/ppermute | solution.py:291
  9.9 14.5 %collective-permute-start.1 = (f32[2,256,256]{2,1,0:T(8,128)}, f32[2,256,256]{2,1,0:T(8,128)S(1)}, u32[]{:S(2)}, u32[]{:S(2)}) collective-permute-start(f32[2,256,256]{2,1,0:T(8,128)} %get-tuple-element.17), channel_id=1, source_target_pairs={{6,5},{2,1},{5,4},{8,7},{7,6},{10,3},{9,11},{11,10},{22,21},{18,17... | collective-permute-start | bytes 1572872 | tf_op jit(solution)/shard_map/ppermute | solution.py:291
  10.6 13.8 %collective-permute-start.2 = (f32[1,256,256]{2,1,0:T(8,128)}, f32[1,256,256]{2,1,0:T(8,128)S(1)}, u32[]{:S(2)}, u32[]{:S(2)}) collective-permute-start(f32[1,256,256]{2,1,0:T(8,128)} %get-tuple-element.18), channel_id=1, source_target_pairs={{3,0},{7,1},{4,2},{5,3},{9,8},{8,9},{10,6},{12,11},{13,10},{14,7},... | collective-permute-start | bytes 786440 | tf_op jit(solution)/shard_map/ppermute | solution.py:291
  11.9 14.4 %copy-start.7 = (f32[1,256,256]{2,1,0:T(8,128)S(1)}, f32[1,256,256]{2,1,0:T(8,128)}, u32[]{:S(2)}) copy-start(f32[1,256,256]{2,1,0:T(8,128)} %get-tuple-element.22) | copy-start | bytes 786436
  11.9 17.1 %copy-start.6 = (s32[1,1,256]{2,1,0:T(1,128)S(1)}, s32[1,1,256]{2,1,0:T(1,128)}, u32[]{:S(2)}) copy-start(s32[1,1,256]{2,1,0:T(1,128)} %param.11) | copy-start | bytes 3076
  11.9 18.4 %copy-start.8 = (f32[64]{0:T(128)S(1)}, f32[64]{0:T(128)}, u32[]{:S(2)}) copy-start(f32[64]{0:T(128)} %param.13) | copy-start | bytes 772
  12.0 18.5 %copy-start.2 = (f32[1,1,7,256,256]{4,3,2,1,0:T(8,128)S(1)}, f32[1,1,7,256,256]{4,3,2,1,0:T(8,128)}, u32[]{:S(2)}) copy-start(f32[1,1,7,256,256]{4,3,2,1,0:T(8,128)} %param.10) | copy-start | bytes 5505028
  12.0 18.4 %copy-start.3 = (s32[1,1,256,256]{3,2,1,0:T(8,128)S(1)}, s32[1,1,256,256]{3,2,1,0:T(8,128)}, u32[]{:S(2)}) copy-start(s32[1,1,256,256]{3,2,1,0:T(8,128)} %param.12) | copy-start | bytes 786436
  12.0 18.8 %collective-permute-start.3 = (f32[1,256,256]{2,1,0:T(8,128)}, f32[1,256,256]{2,1,0:T(8,128)S(1)}, u32[]{:S(2)}, u32[]{:S(2)}) collective-permute-start(f32[1,256,256]{2,1,0:T(8,128)} %get-tuple-element.19), channel_id=1, source_target_pairs={{4,0},{8,1},{6,2},{9,3},{7,4},{10,5},{11,6},{20,16},{24,17},{22,18... | collective-permute-start | bytes 786440 | tf_op jit(solution)/shard_map/ppermute | solution.py:291
  26.3 8.4 %copy-start.1 = (f32[1,1,7,256,256]{4,3,2,1,0:T(8,128)S(1)}, f32[1,1,7,256,256]{4,3,2,1,0:T(8,128)}, u32[]{:S(2)}) copy-start(f32[1,1,7,256,256]{4,3,2,1,0:T(8,128)} %param.8) | copy-start | bytes 5505028
  26.3 8.4 %copy-start.4 = (s32[7,16]{1,0:T(8,128)S(1)}, s32[7,16]{1,0:T(8,128)}, u32[]{:S(2)}) copy-start(s32[7,16]{1,0:T(8,128)} %constant.8.clone.table_ref) | copy-start | bytes 1348
  26.3 8.4 %collective-permute-start.5 = (f32[1,256,256]{2,1,0:T(8,128)S(1)}, f32[1,256,256]{2,1,0:T(8,128)S(1)}, u32[]{:S(2)}, u32[]{:S(2)}) collective-permute-start(f32[1,256,256]{2,1,0:T(8,128)S(1)} %copy-done.7), channel_id=1, source_target_pairs={{2,0},{3,1},{5,2},{4,3},{10,4},{11,5},{12,7},{18,16},{19,17},{21,1... | collective-permute-start | bytes 786440 | tf_op jit(solution)/shard_map/ppermute | solution.py:307
  27.8 19.8 %collective-permute-start.6 = (f32[264,256]{1,0:T(8,128)S(1)}, f32[264,256]{1,0:T(8,128)S(1)}, u32[]{:S(2)}, u32[]{:S(2)}) collective-permute-start(f32[264,256]{1,0:T(8,128)S(1)} %far.1), channel_id=1, source_target_pairs={{5,0},{4,1},{7,2},{6,3},{8,4},{9,5},{11,6},{10,7},{21,16},{20,17},... | collective-permute-start | bytes 811016 | tf_op jit(solution)/shard_map/ppermute | solution.py:306
  29.1 16.3 %collective-permute-start.7 = (s32[1,256]{1,0:T(1,128)S(1)}, s32[1,256]{1,0:T(1,128)S(1)}, u32[]{:S(2)}, u32[]{:S(2)}) collective-permute-start(s32[1,256]{1,0:T(1,128)S(1)} %bitcast.17), channel_id=1, source_target_pairs={{8,0},{9,1},{10,2},{11,3},{12,4},{13,5},{14,6},{15,7},{24,16},{25,... | collective-permute-start | bytes 3080 | tf_op jit(solution)/shard_map/ppermute | solution.py:293

commit v3 on v2

--- a/solution.py
+++ b/solution.py
@@ -13,16 +13,15 @@
 LANES = 128
 FIRST = 1
 LATE = 4
-GATE = 1
 PLAN = (
-    (5, (5, 6, 7), (0, 4, 2, 3, -1, 1, 0)),
-    (3, (3, 4, 5), (1, 4, -1, 1, 0, 2, 3)),
-    (5, (5, 6, 7), (0, 2, 4, 3, -1, 1, 0)),
-    (3, (3, 4, 5), (4, 2, -1, 1, 0, 3, 1)),
-    (4, (4, 5, 7), (1, 0, 3, -1, 2, 4, 0)),
-    (4, (3, 4, 7), (1, 0, 2, -1, 3, 4, 0)),
-    (5, (3, 6, 7), (1, 0, 1, 2, 3, 2, 0)),
-    (3, (3, 4, 6), (1, 0, -1, 1, 4, 2, 2)),
+    (5, (5, 6, 7), (4, 1, 2, 3, -1, 1, 0)),
+    (3, (3, 4, 5), (4, 0, -1, 1, 0, 2, 3)),
+    (5, (5, 6, 7), (1, 0, 2, 3, -1, 1, 0)),
+    (3, (3, 4, 5), (2, 3, -1, 1, 0, 4, 1)),
+    (4, (4, 5, 7), (1, 0, 3, -1, 2, 4, 1)),
+    (4, (3, 4, 7), (1, 0, 2, -1, 3, 4, 1)),
+    (5, (3, 6, 7), (1, 0, 1, 2, 3, 0, 2)),
+    (3, (3, 4, 6), (1, 0, -1, 2, 4, 0, 2)),
 )
 
 
@@ -284,7 +283,11 @@
 
     picked = pick("pick_first", (qm, qm1), (plan.moved, plan.send[:cut]), tuple(stack[:first + 1]))
     left, blocks = picked[0], picked[1:]
-    blocks += pick("pick_rest", (qm1,), (plan.send[cut:],), tuple(stack[first + 1:]))
+    mid = min(LATE, rounds)
+    end = plan.starts[mid]
+    blocks += pick("pick_rest", (qm1,), (plan.send[cut:end],), tuple(stack[first + 1:mid + 1]))
+    if rounds > mid:
+        blocks += pick("pick_late", (qm1,), (plan.send[end:],), tuple(stack[mid + 1:]))
     left = lax.ppermute(left, "row", plan.there)
     early = [t for t in range(rounds) if t < LATE or t in plan.far_rounds]
     late = [t for t in range(rounds) if t not in early]
@@ -299,7 +302,7 @@
         functools.partial(far_kernel, plan, dist), "far", tall, [smem] + [vmem] * (2 + len(plan.far_rounds)),
         (jnp.asarray(plan.far), qm1, left, *(rights[t] for t in plan.far_rounds)), 3,
     )
-    if late and GATE:
+    if late:
         held, far = lax.optimization_barrier(([blocks[t] for t in late], far))
     else:
         held = [blocks[t] for t in late]

time: 49.4 us -> 48.8 us (0.988)
  the two profiles are of different devices: /device:TPU:0 before, /device:TPU:5 now
where the time goes in v3:
time: 48.8 us; the launch traced here: 48.5 us
  waiting for transfers between devices  22.4 us (46%)
  starting transfers between devices  15.2 us (31%)
  Pallas kernels  9.89 us (20%)
  between operations  0.86 us (2%)
    ppermute x4, waiting for transfers between devices, per_device(): rights = {t: lax.ppermute(blocks[t], 'row', plan.pairs[t]) for t in early}  10.9 us
    pallas_call x7, Pallas kernels, call(): pl.pallas_call(kernel, out_shape=outs, in_specs=ins, out_specs=(vmem,) *...  9.89 us
    ppermute x1, waiting for transfers between devices, per_device(): lax.ppermute(block, 'row', plan.pairs[t])  9.79 us
    ppermute x4, starting transfers between devices, per_device(): rights = {t: lax.ppermute(blocks[t], 'row', plan.pairs[t]) for t in early}  7.35 us
    ppermute x1, starting transfers between devices, per_device(): left = lax.ppermute(left, 'row', plan.there)  3.89 us
    ppermute x1, waiting for transfers between devices, per_device(): end = lax.ppermute(own, 'row', [(i + dist, i) for i in range(plan.lives)])  1.7 us
    ppermute x1, starting transfers between devices, per_device(): lax.ppermute(block, 'row', plan.pairs[t])  1.42 us
    ppermute x1, starting transfers between devices, per_device(): far = lax.ppermute(far, 'row', plan.back)  1.29 us
  transfers between devices with their start and end apart: 8, of which 4 were waited for; matrix products, arithmetic and copies ran while one was open for 0% of the time, Pallas kernels for 12%

profile of v3, /device:TPU:5, one launch (start us, length us, event | category | flops | bytes accessed | tf_op | source)
XLA Modules:
  0.0 48.5 jit_solution(18427315233736951770)
XLA Ops:
  0.6 2.3 %pick_first.1 = (f32[3,256,256]{2,1,0:T(8,128)}, f32[2,256,256]{2,1,0:T(8,128)}) custom-call(f32[7,256,256]{2,1,0:T(8,128)} %bitcast.14, f32[7,256,256]{2,1,0:T(8,128)} %bitcast.10), custom_call_target="tpu_custom_call" | custom-call | bytes 2359296 | tf_op jit(solution)/shard_map/pick_first/pallas_call | solution.py:259
  3.0 3.9 %collective-permute-start.4 = (f32[3,256,256]{2,1,0:T(8,128)}, f32[3,256,256]{2,1,0:T(8,128)S(1)}, u32[]{:S(2)}, u32[]{:S(2)}) collective-permute-start(f32[3,256,256]{2,1,0:T(8,128)} %get-tuple-element.19), channel_id=1, source_target_pairs={{0,5},{1,4},{2,7},{3,6},{4,8},{5,9},{6,11},{7,10},{16,21},{17,20},... | collective-permute-start | bytes 2359304 | tf_op jit(solution)/shard_map/ppermute | solution.py:291
  6.9 0.0 copy-start
  6.9 0.0 copy-start.5
  6.9 2.2 %collective-permute-start = (f32[2,256,256]{2,1,0:T(8,128)}, f32[2,256,256]{2,1,0:T(8,128)S(1)}, u32[]{:S(2)}, u32[]{:S(2)}) collective-permute-start(f32[2,256,256]{2,1,0:T(8,128)} %get-tuple-element.15), channel_id=1, source_target_pairs={{7,5},{3,1},{6,4},{4,2},{9,7},{8,6},{12,11},{13,10},{23,21},{19,17... | collective-permute-start | bytes 1572872 | tf_op jit(solution)/shard_map/ppermute | solution.py:294
  9.1 2.0 %pick_rest.1 = (f32[2,256,256]{2,1,0:T(8,128)}, f32[1,256,256]{2,1,0:T(8,128)}, f32[1,256,256]{2,1,0:T(8,128)}) custom-call(f32[7,256,256]{2,1,0:T(8,128)} %bitcast.11), custom_call_target="tpu_custom_call" | custom-call | bytes 2359296 | tf_op jit(solution)/shard_map/pick_rest/pallas_call | solution.py:259
  11.2 1.9 %collective-permute-start.1 = (f32[2,256,256]{2,1,0:T(8,128)}, f32[2,256,256]{2,1,0:T(8,128)S(1)}, u32[]{:S(2)}, u32[]{:S(2)}) collective-permute-start(f32[2,256,256]{2,1,0:T(8,128)} %get-tuple-element.16), channel_id=1, source_target_pairs={{2,0},{6,5},{5,4},{3,2},{8,7},{7,6},{10,3},{11,8},{12,9},{9,11},{1... | collective-permute-start | bytes 1572872 | tf_op jit(solution)/shard_map/ppermute | solution.py:294
  13.1 1.9 %collective-permute-start.2 = (f32[1,256,256]{2,1,0:T(8,128)}, f32[1,256,256]{2,1,0:T(8,128)S(1)}, u32[]{:S(2)}, u32[]{:S(2)}) collective-permute-start(f32[1,256,256]{2,1,0:T(8,128)} %get-tuple-element.17), channel_id=1, source_target_pairs={{3,0},{7,1},{5,2},{4,3},{9,8},{8,9},{10,6},{13,11},{11,10},{14,7},... | collective-permute-start | bytes 786440 | tf_op jit(solution)/shard_map/ppermute | solution.py:294
  15.0 1.3 %collective-permute-start.3 = (f32[1,256,256]{2,1,0:T(8,128)}, f32[1,256,256]{2,1,0:T(8,128)}, u32[]{:S(2)}, u32[]{:S(2)}) collective-permute-start(f32[1,256,256]{2,1,0:T(8,128)} %get-tuple-element.18), channel_id=1, source_target_pairs={{4,0},{8,1},{6,2},{5,3},{7,4},{10,5},{11,6},{20,16},{24,17},{22,18... | collective-permute-start | bytes 786440 | tf_op jit(solution)/shard_map/ppermute | solution.py:294
  16.3 0.7 %pick_late.1 = f32[1,256,256]{2,1,0:T(8,128)} custom-call(f32[7,256,256]{2,1,0:T(8,128)} %bitcast.12), custom_call_target="tpu_custom_call" | custom-call | bytes 2359296 | tf_op jit(solution)/shard_map/pick_late/pallas_call | solution.py:259
  17.1 0.0 copy-start.7
  17.1 0.0 copy-start.6
  17.1 0.0 copy-start.8
  17.1 0.0 copy-start.2
  17.1 0.0 copy-start.3
  17.1 8.4 %collective-permute-done.2.refs_2_ = f32[1,256,256]{2,1,0:T(8,128)S(1)} collective-permute-done((f32[1,256,256]{2,1,0:T(8,128)}, f32[1,256,256]{2,1,0:T(8,128)S(1)}, u32[]{:S(2)}, u32[]{:S(2)}) %collective-permute-start.2) | collective-permute-done | bytes 262176 | tf_op jit(solution)/shard_map/ppermute | solution.py:294
  25.5 0.0 collective-permute-done.refs_0_
  25.5 2.5 %collective-permute-done.1.refs_1_ = f32[2,256,256]{2,1,0:T(8,128)S(1)} collective-permute-done((f32[2,256,256]{2,1,0:T(8,128)}, f32[2,256,256]{2,1,0:T(8,128)S(1)}, u32[]{:S(2)}, u32[]{:S(2)}) %collective-permute-start.1) | collective-permute-done | bytes 524320 | tf_op jit(solution)/shard_map/ppermute | solution.py:294
  28.0 0.0 collective-permute-done.4.left_ref
  28.0 0.0 copy-done
  28.1 0.0 copy-done.5
  28.1 0.6 %far.1 = f32[264,256]{1,0:T(8,128)S(1)} custom-call(s32[7,16]{1,0:T(8,128)S(1)} %copy-done.5, f32[7,256,256]{2,1,0:T(8,128)S(1)} %bitcast.13, f32[3,256,256]{2,1,0:T(8,128)S(1)} %collective-permute-done.4.left_ref, f32[2,256,256]{2,1,0:T(8,128)S(1)} %collective-permute-done.refs_0_, f32[2,256,256]{2,1,0:T(8,128)S(1)} %collective-permute-done.1.refs_1_, ...), custom_call_target="tpu_custom_call" | custom-call | flops 301989888 | bytes 2359296 | tf_op jit(solution)/shard_map/far/pallas_call | solution.py:259
  28.7 0.0 copy-done.7
  28.7 0.0 copy-start.1
  28.7 0.0 copy-start.4
  28.7 1.4 %collective-permute-start.5 = (f32[1,256,256]{2,1,0:T(8,128)S(1)}, f32[1,256,256]{2,1,0:T(8,128)S(1)}, u32[]{:S(2)}, u32[]{:S(2)}) collective-permute-start(f32[1,256,256]{2,1,0:T(8,128)S(1)} %copy-done.7), channel_id=1, source_target_pairs={{1,0},{2,1},{9,3},{10,4},{11,5},{12,7},{17,16},{18,17},{25,19},{26... | collective-permute-start | bytes 786440 | tf_op jit(solution)/shard_map/ppermute | solution.py:310
  30.2 1.3 %collective-permute-start.6 = (f32[264,256]{1,0:T(8,128)S(1)}, f32[264,256]{1,0:T(8,128)S(1)}, u32[]{:S(2)}, u32[]{:S(2)}) collective-permute-start(f32[264,256]{1,0:T(8,128)S(1)} %far.1), channel_id=1, source_target_pairs={{5,0},{4,1},{7,2},{6,3},{8,4},{9,5},{11,6},{10,7},{21,16},{20,17},... | collective-permute-start | bytes 811016 | tf_op jit(solution)/shard_map/ppermute | solution.py:309
  31.5 0.0 copy-done.6
  31.5 1.3 %collective-permute-start.7 = (s32[1,256]{1,0:T(1,128)S(1)}, s32[1,256]{1,0:T(1,128)S(1)}, u32[]{:S(2)}, u32[]{:S(2)}) collective-permute-start(s32[1,256]{1,0:T(1,128)S(1)} %bitcast.18), channel_id=1, source_target_pairs={{8,0},{9,1},{10,2},{11,3},{12,4},{13,5},{14,6},{15,7},{24,16},{25,... | collective-permute-start | bytes 3080 | tf_op jit(solution)/shard_map/ppermute | solution.py:296
  32.8 0.0 copy-done.8
  32.8 0.0 copy-done.2
  32.8 0.0 copy-done.3
  32.8 0.3 weights.1
  33.2 0.0 collective-permute-done.3.refs_3_
  33.2 9.8 %collective-permute-done.5.refs_4_ = f32[1,256,256]{2,1,0:T(8,128)S(1)} collective-permute-done((f32[1,256,256]{2,1,0:T(8,128)S(1)}, f32[1,256,256]{2,1,0:T(8,128)S(1)}, u32[]{:S(2)}, u32[]{:S(2)}) %collective-permute-start.5) | collective-permute-done | bytes 262176 | tf_op jit(solution)/shard_map/ppermute | solution.py:310
  43.0 0.0 copy-done.1
  43.0 0.0 copy-done.4
  43.0 2.3 %near.1.near_ref = f32[264,256]{1,0:T(8,128)S(1)} custom-call(s32[7,16]{1,0:T(8,128)S(1)} %copy-done.4, f32[7,256,256]{2,1,0:T(8,128)S(1)} %bitcast.15, f32[2,256,256]{2,1,0:T(8,128)S(1)} %collective-permute-done.refs_0_, f32[2,256,256]{2,1,0:T(8,128)S(1)} %collective-permute-done.1.refs_1_, f32[1,256,256]{2,1,0:T(8,128)S(1)} %collective-permute-done.2.refs_2_, ...), custom_call_target="tpu_custom_call" | custom-call | flops 704643072 | bytes 2359296 | tf_op jit(solution)/shard_map/near/pallas_call | solution.py:259
  45.2 1.7 %collective-permute-done.7.end_ref = s32[1,256]{1,0:T(1,128)S(1)} collective-permute-done((s32[1,256]{1,0:T(1,128)S(1)}, s32[1,256]{1,0:T(1,128)S(1)}, u32[]{:S(2)}, u32[]{:S(2)}) %collective-permute-start.7) | collective-permute-done | bytes 1056 | tf_op jit(solution)/shard_map/ppermute | solution.py:296
  46.9 0.0 collective-permute-done.6.far_ref
  47.0 1.5 %last.1 = (f32[256,256]{1,0:T(8,128)}, f32[256,256]{1,0:T(8,128)}, f32[256,256]{1,0:T(8,128)}) custom-call(f32[264,256]{1,0:T(8,128)S(1)} %near.1.near_ref, f32[264,256]{1,0:T(8,128)S(1)} %collective-permute-done.6.far_ref, f32[256,256]{1,0:T(8,128)S(1)} %get-tuple-element.22.weight_ref, f32[256,1]{1,0:T(8,128)S(1)} %get-tuple-element.23.branch_ref, ...), custom_call_target="tpu_custom_call" | custom-call | flops 201326592 | bytes 2359296 | tf_op jit(solution)/shard_map/last/pallas_call | solution.py:259
  (1 shorter events, 0.0 us)
Async XLA Ops:
  3.0 25.1 %collective-permute-start.4 = (f32[3,256,256]{2,1,0:T(8,128)}, f32[3,256,256]{2,1,0:T(8,128)S(1)}, u32[]{:S(2)}, u32[]{:S(2)}) collective-permute-start(f32[3,256,256]{2,1,0:T(8,128)} %get-tuple-element.19), channel_id=1, source_target_pairs={{0,5},{1,4},{2,7},{3,6},{4,8},{5,9},{6,11},{7,10},{16,21},{17,20},... | collective-permute-start | bytes 2359304 | tf_op jit(solution)/shard_map/ppermute | solution.py:291
  6.9 21.2 %copy-start = (f32[1,1,7,256,256]{4,3,2,1,0:T(8,128)S(1)}, f32[1,1,7,256,256]{4,3,2,1,0:T(8,128)}, u32[]{:S(2)}) copy-start(f32[1,1,7,256,256]{4,3,2,1,0:T(8,128)} %param.9) | copy-start | bytes 5505028
  6.9 21.2 %copy-start.5 = (s32[7,16]{1,0:T(8,128)S(1)}, s32[7,16]{1,0:T(8,128)}, u32[]{:S(2)}) copy-start(s32[7,16]{1,0:T(8,128)} %constant.7.clone.table_ref) | copy-start | bytes 1348
  6.9 18.6 %collective-permute-start = (f32[2,256,256]{2,1,0:T(8,128)}, f32[2,256,256]{2,1,0:T(8,128)S(1)}, u32[]{:S(2)}, u32[]{:S(2)}) collective-permute-start(f32[2,256,256]{2,1,0:T(8,128)} %get-tuple-element.15), channel_id=1, source_target_pairs={{7,5},{3,1},{6,4},{4,2},{9,7},{8,6},{12,11},{13,10},{23,21},{19,17... | collective-permute-start | bytes 1572872 | tf_op jit(solution)/shard_map/ppermute | solution.py:294
  11.2 16.9 %collective-permute-start.1 = (f32[2,256,256]{2,1,0:T(8,128)}, f32[2,256,256]{2,1,0:T(8,128)S(1)}, u32[]{:S(2)}, u32[]{:S(2)}) collective-permute-start(f32[2,256,256]{2,1,0:T(8,128)} %get-tuple-element.16), channel_id=1, source_target_pairs={{2,0},{6,5},{5,4},{3,2},{8,7},{7,6},{10,3},{11,8},{12,9},{9,11},{1... | collective-permute-start | bytes 1572872 | tf_op jit(solution)/shard_map/ppermute | solution.py:294
  13.1 12.4 %collective-permute-start.2 = (f32[1,256,256]{2,1,0:T(8,128)}, f32[1,256,256]{2,1,0:T(8,128)S(1)}, u32[]{:S(2)}, u32[]{:S(2)}) collective-permute-start(f32[1,256,256]{2,1,0:T(8,128)} %get-tuple-element.17), channel_id=1, source_target_pairs={{3,0},{7,1},{5,2},{4,3},{9,8},{8,9},{10,6},{13,11},{11,10},{14,7},... | collective-permute-start | bytes 786440 | tf_op jit(solution)/shard_map/ppermute | solution.py:294
  15.0 18.1 %collective-permute-start.3 = (f32[1,256,256]{2,1,0:T(8,128)}, f32[1,256,256]{2,1,0:T(8,128)}, u32[]{:S(2)}, u32[]{:S(2)}) collective-permute-start(f32[1,256,256]{2,1,0:T(8,128)} %get-tuple-element.18), channel_id=1, source_target_pairs={{4,0},{8,1},{6,2},{5,3},{7,4},{10,5},{11,6},{20,16},{24,17},{22,18... | collective-permute-start | bytes 786440 | tf_op jit(solution)/shard_map/ppermute | solution.py:294
  17.1 11.6 %copy-start.7 = (f32[1,256,256]{2,1,0:T(8,128)S(1)}, f32[1,256,256]{2,1,0:T(8,128)}, u32[]{:S(2)}) copy-start(f32[1,256,256]{2,1,0:T(8,128)} %pick_late.1) | copy-start | bytes 786436
  17.1 14.4 %copy-start.6 = (s32[1,1,256]{2,1,0:T(1,128)S(1)}, s32[1,1,256]{2,1,0:T(1,128)}, u32[]{:S(2)}) copy-start(s32[1,1,256]{2,1,0:T(1,128)} %param.11) | copy-start | bytes 3076
  17.1 15.7 %copy-start.8 = (f32[64]{0:T(128)S(1)}, f32[64]{0:T(128)}, u32[]{:S(2)}) copy-start(f32[64]{0:T(128)} %param.13) | copy-start | bytes 772
  17.1 15.7 %copy-start.2 = (f32[1,1,7,256,256]{4,3,2,1,0:T(8,128)S(1)}, f32[1,1,7,256,256]{4,3,2,1,0:T(8,128)}, u32[]{:S(2)}) copy-start(f32[1,1,7,256,256]{4,3,2,1,0:T(8,128)} %param.10) | copy-start | bytes 5505028
  17.1 15.7 %copy-start.3 = (s32[1,1,256,256]{3,2,1,0:T(8,128)S(1)}, s32[1,1,256,256]{3,2,1,0:T(8,128)}, u32[]{:S(2)}) copy-start(s32[1,1,256,256]{3,2,1,0:T(8,128)} %param.12) | copy-start | bytes 786436
  28.7 14.2 %copy-start.1 = (f32[1,1,7,256,256]{4,3,2,1,0:T(8,128)S(1)}, f32[1,1,7,256,256]{4,3,2,1,0:T(8,128)}, u32[]{:S(2)}) copy-start(f32[1,1,7,256,256]{4,3,2,1,0:T(8,128)} %param.8) | copy-start | bytes 5505028
  28.7 14.2 %copy-start.4 = (s32[7,16]{1,0:T(8,128)S(1)}, s32[7,16]{1,0:T(8,128)}, u32[]{:S(2)}) copy-start(s32[7,16]{1,0:T(8,128)} %constant.8.clone.table_ref) | copy-start | bytes 1348
  28.7 14.2 %collective-permute-start.5 = (f32[1,256,256]{2,1,0:T(8,128)S(1)}, f32[1,256,256]{2,1,0:T(8,128)S(1)}, u32[]{:S(2)}, u32[]{:S(2)}) collective-permute-start(f32[1,256,256]{2,1,0:T(8,128)S(1)} %copy-done.7), channel_id=1, source_target_pairs={{1,0},{2,1},{9,3},{10,4},{11,5},{12,7},{17,16},{18,17},{25,19},{26... | collective-permute-start | bytes 786440 | tf_op jit(solution)/shard_map/ppermute | solution.py:310
  30.2 16.8 %collective-permute-start.6 = (f32[264,256]{1,0:T(8,128)S(1)}, f32[264,256]{1,0:T(8,128)S(1)}, u32[]{:S(2)}, u32[]{:S(2)}) collective-permute-start(f32[264,256]{1,0:T(8,128)S(1)} %far.1), channel_id=1, source_target_pairs={{5,0},{4,1},{7,2},{6,3},{8,4},{9,5},{11,6},{10,7},{21,16},{20,17},... | collective-permute-start | bytes 811016 | tf_op jit(solution)/shard_map/ppermute | solution.py:309
  31.5 15.5 %collective-permute-start.7 = (s32[1,256]{1,0:T(1,128)S(1)}, s32[1,256]{1,0:T(1,128)S(1)}, u32[]{:S(2)}, u32[]{:S(2)}) collective-permute-start(s32[1,256]{1,0:T(1,128)S(1)} %bitcast.18), channel_id=1, source_target_pairs={{8,0},{9,1},{10,2},{11,3},{12,4},{13,5},{14,6},{15,7},{24,16},{25,... | collective-permute-start | bytes 3080 | tf_op jit(solution)/shard_map/ppermute | solution.py:296

commit v4 on v3

--- a/solution.py
+++ b/solution.py
@@ -310,7 +310,7 @@
     rights.update((t, lax.ppermute(block, "row", plan.pairs[t])) for t, block in zip(late, held))
     near = call(
         functools.partial(near_kernel, plan, dist), "near", tall, [smem] + [vmem] * (1 + rounds),
-        (jnp.asarray(plan.near), qm, *(rights[t] for t in range(rounds))), 7,
+        (jnp.asarray(plan.near), qm, *(rights[t] for t in range(rounds))), 20,
     )
     pair, branch, out = call(
         functools.partial(last_kernel, plan, dist), "last", (square,) * 3, [vmem] * 6,

time: 48.8 us -> 47.9 us (0.982)
  the two profiles are of different devices: /device:TPU:5 before, /device:TPU:0 now
where the time goes in v4:
time: 47.9 us; the launch traced here: 47.5 us
  waiting for transfers between devices  24.7 us (52%)
  starting transfers between devices  13.1 us (27%)
  Pallas kernels  8.78 us (18%)
  between operations  0.88 us (2%)
    ppermute x4, waiting for transfers between devices, per_device(): rights = {t: lax.ppermute(blocks[t], 'row', plan.pairs[t]) for t in early}  15.5 us
    pallas_call x7, Pallas kernels, call(): pl.pallas_call(kernel, out_shape=outs, in_specs=ins, out_specs=(vmem,) *...  8.78 us
    ppermute x1, waiting for transfers between devices, per_device(): far = lax.ppermute(far, 'row', plan.back)  8.07 us
    ppermute x4, starting transfers between devices, per_device(): rights = {t: lax.ppermute(blocks[t], 'row', plan.pairs[t]) for t in early}  4.7 us
    ppermute x1, starting transfers between devices, per_device(): left = lax.ppermute(left, 'row', plan.there)  4.42 us
    ppermute x1, starting transfers between devices, per_device(): lax.ppermute(block, 'row', plan.pairs[t])  1.42 us
    ppermute x1, starting transfers between devices, per_device(): end = lax.ppermute(own, 'row', [(i + dist, i) for i in range(plan.lives)])  1.29 us
    ppermute x1, starting transfers between devices, per_device(): far = lax.ppermute(far, 'row', plan.back)  1.29 us
  transfers between devices with their start and end apart: 8, of which 4 were waited for; matrix products, arithmetic and copies ran while one was open for 0% of the time, Pallas kernels for 11%

profile of v4, /device:TPU:0, one launch (start us, length us, event | category | flops | bytes accessed | tf_op | source)
XLA Modules:
  0.0 47.5 jit_solution(8228587390802071625)
XLA Ops:
  0.6 2.3 %pick_first.1 = (f32[3,256,256]{2,1,0:T(8,128)}, f32[2,256,256]{2,1,0:T(8,128)}) custom-call(f32[7,256,256]{2,1,0:T(8,128)} %bitcast.14, f32[7,256,256]{2,1,0:T(8,128)} %bitcast.10), custom_call_target="tpu_custom_call" | custom-call | bytes 2359296 | tf_op jit(solution)/shard_map/pick_first/pallas_call | solution.py:259
  2.9 4.4 %collective-permute-start.4 = (f32[3,256,256]{2,1,0:T(8,128)}, f32[3,256,256]{2,1,0:T(8,128)S(1)}, u32[]{:S(2)}, u32[]{:S(2)}) collective-permute-start(f32[3,256,256]{2,1,0:T(8,128)} %get-tuple-element.19), channel_id=1, source_target_pairs={{0,5},{1,4},{2,7},{3,6},{4,8},{5,9},{6,11},{7,10},{16,21},{17,20},... | collective-permute-start | bytes 2359304 | tf_op jit(solution)/shard_map/ppermute | solution.py:291
  7.3 0.0 copy-start
  7.3 0.0 copy-start.4
  7.3 0.8 %collective-permute-start = (f32[2,256,256]{2,1,0:T(8,128)}, f32[2,256,256]{2,1,0:T(8,128)S(1)}, u32[]{:S(2)}, u32[]{:S(2)}) collective-permute-start(f32[2,256,256]{2,1,0:T(8,128)} %get-tuple-element.15), channel_id=1, source_target_pairs={{7,5},{3,1},{6,4},{4,2},{9,7},{8,6},{12,11},{13,10},{23,21},{19,17... | collective-permute-start | bytes 1572872 | tf_op jit(solution)/shard_map/ppermute | solution.py:294
  8.2 1.0 %pick_rest.1 = (f32[2,256,256]{2,1,0:T(8,128)}, f32[1,256,256]{2,1,0:T(8,128)}, f32[1,256,256]{2,1,0:T(8,128)}) custom-call(f32[7,256,256]{2,1,0:T(8,128)} %bitcast.11), custom_call_target="tpu_custom_call" | custom-call | bytes 2359296 | tf_op jit(solution)/shard_map/pick_rest/pallas_call | solution.py:259
  9.2 1.3 %collective-permute-start.1 = (f32[2,256,256]{2,1,0:T(8,128)}, f32[2,256,256]{2,1,0:T(8,128)S(1)}, u32[]{:S(2)}, u32[]{:S(2)}) collective-permute-start(f32[2,256,256]{2,1,0:T(8,128)} %get-tuple-element.16), channel_id=1, source_target_pairs={{2,0},{6,5},{5,4},{3,2},{8,7},{7,6},{10,3},{11,8},{12,9},{9,11},{1... | collective-permute-start | bytes 1572872 | tf_op jit(solution)/shard_map/ppermute | solution.py:294
  10.5 1.3 %collective-permute-start.2 = (f32[1,256,256]{2,1,0:T(8,128)}, f32[1,256,256]{2,1,0:T(8,128)S(1)}, u32[]{:S(2)}, u32[]{:S(2)}) collective-permute-start(f32[1,256,256]{2,1,0:T(8,128)} %get-tuple-element.17), channel_id=1, source_target_pairs={{3,0},{7,1},{5,2},{4,3},{9,8},{8,9},{10,6},{13,11},{11,10},{14,7},... | collective-permute-start | bytes 786440 | tf_op jit(solution)/shard_map/ppermute | solution.py:294
  11.8 1.3 %collective-permute-start.3 = (f32[1,256,256]{2,1,0:T(8,128)}, f32[1,256,256]{2,1,0:T(8,128)}, u32[]{:S(2)}, u32[]{:S(2)}) collective-permute-start(f32[1,256,256]{2,1,0:T(8,128)} %get-tuple-element.18), channel_id=1, source_target_pairs={{4,0},{8,1},{6,2},{5,3},{7,4},{10,5},{11,6},{20,16},{24,17},{22,18... | collective-permute-start | bytes 786440 | tf_op jit(solution)/shard_map/ppermute | solution.py:294
  13.1 0.7 %pick_late.1 = f32[1,256,256]{2,1,0:T(8,128)} custom-call(f32[7,256,256]{2,1,0:T(8,128)} %bitcast.12), custom_call_target="tpu_custom_call" | custom-call | bytes 2359296 | tf_op jit(solution)/shard_map/pick_late/pallas_call | solution.py:259
  13.9 0.0 copy-start.7
  13.9 0.0 copy-start.5
  13.9 0.0 copy-start.8
  13.9 0.0 copy-start.2
  13.9 0.0 copy-start.3
  13.9 14.9 %collective-permute-done.2.refs_2_ = f32[1,256,256]{2,1,0:T(8,128)S(1)} collective-permute-done((f32[1,256,256]{2,1,0:T(8,128)}, f32[1,256,256]{2,1,0:T(8,128)S(1)}, u32[]{:S(2)}, u32[]{:S(2)}) %collective-permute-start.2) | collective-permute-done | bytes 262176 | tf_op jit(solution)/shard_map/ppermute | solution.py:294
  28.8 0.0 collective-permute-done.refs_0_
  28.8 0.5 %collective-permute-done.1.refs_1_ = f32[2,256,256]{2,1,0:T(8,128)S(1)} collective-permute-done((f32[2,256,256]{2,1,0:T(8,128)}, f32[2,256,256]{2,1,0:T(8,128)S(1)}, u32[]{:S(2)}, u32[]{:S(2)}) %collective-permute-start.1) | collective-permute-done | bytes 524320 | tf_op jit(solution)/shard_map/ppermute | solution.py:294
  29.4 0.0 collective-permute-done.4.left_ref
  29.4 0.0 copy-done
  29.4 0.0 copy-done.4
  29.4 0.6 %far.1 = f32[264,256]{1,0:T(8,128)S(1)} custom-call(s32[7,16]{1,0:T(8,128)S(1)} %copy-done.4, f32[7,256,256]{2,1,0:T(8,128)S(1)} %bitcast.13, f32[3,256,256]{2,1,0:T(8,128)S(1)} %collective-permute-done.4.left_ref, f32[2,256,256]{2,1,0:T(8,128)S(1)} %collective-permute-done.refs_0_, f32[2,256,256]{2,1,0:T(8,128)S(1)} %collective-permute-done.1.refs_1_, ...), custom_call_target="tpu_custom_call" | custom-call | flops 301989888 | bytes 2359296 | tf_op jit(solution)/shard_map/far/pallas_call | solution.py:259
  30.0 0.0 copy-done.7
  30.1 0.0 copy-start.1
  30.1 0.0 copy-start.6
  30.1 1.4 %collective-permute-start.5 = (f32[1,256,256]{2,1,0:T(8,128)S(1)}, f32[1,256,256]{2,1,0:T(8,128)S(1)}, u32[]{:S(2)}, u32[]{:S(2)}) collective-permute-start(f32[1,256,256]{2,1,0:T(8,128)S(1)} %copy-done.7), channel_id=1, source_target_pairs={{1,0},{2,1},{9,3},{10,4},{11,5},{12,7},{17,16},{18,17},{25,19},{26... | collective-permute-start | bytes 786440 | tf_op jit(solution)/shard_map/ppermute | solution.py:310
  31.5 0.0 copy-done.5
  31.5 1.3 %collective-permute-start.7 = (s32[1,256]{1,0:T(1,128)S(1)}, s32[1,256]{1,0:T(1,128)S(1)}, u32[]{:S(2)}, u32[]{:S(2)}) collective-permute-start(s32[1,256]{1,0:T(1,128)S(1)} %bitcast.18), channel_id=1, source_target_pairs={{8,0},{9,1},{10,2},{11,3},{12,4},{13,5},{14,6},{15,7},{24,16},{25,... | collective-permute-start | bytes 3080 | tf_op jit(solution)/shard_map/ppermute | solution.py:296
  32.8 1.3 %collective-permute-start.6 = (f32[264,256]{1,0:T(8,128)S(1)}, f32[264,256]{1,0:T(8,128)S(1)}, u32[]{:S(2)}, u32[]{:S(2)}) collective-permute-start(f32[264,256]{1,0:T(8,128)S(1)} %far.1), channel_id=1, source_target_pairs={{5,0},{4,1},{7,2},{6,3},{8,4},{9,5},{11,6},{10,7},{21,16},{20,17},... | collective-permute-start | bytes 811016 | tf_op jit(solution)/shard_map/ppermute | solution.py:309
  34.1 0.0 copy-done.8
  34.1 0.0 copy-done.2
  34.2 0.0 copy-done.3
  34.2 0.3 weights.1
  34.5 0.0 collective-permute-done.3.refs_3_
  34.5 0.0 collective-permute-done.5.refs_4_
  34.5 0.0 copy-done.1
  34.5 0.0 copy-done.6
  34.5 2.3 %near.1.near_ref = f32[264,256]{1,0:T(8,128)S(1)} custom-call(s32[7,16]{1,0:T(8,128)S(1)} %copy-done.6, f32[7,256,256]{2,1,0:T(8,128)S(1)} %bitcast.15, f32[2,256,256]{2,1,0:T(8,128)S(1)} %collective-permute-done.refs_0_, f32[2,256,256]{2,1,0:T(8,128)S(1)} %collective-permute-done.1.refs_1_, f32[1,256,256]{2,1,0:T(8,128)S(1)} %collective-permute-done.2.refs_2_, ...), custom_call_target="tpu_custom_call" | custom-call | flops 2013265920 | bytes 2359296 | tf_op jit(solution)/shard_map/near/pallas_call | solution.py:259
  36.8 1.1 %collective-permute-done.7.end_ref = s32[1,256]{1,0:T(1,128)S(1)} collective-permute-done((s32[1,256]{1,0:T(1,128)S(1)}, s32[1,256]{1,0:T(1,128)S(1)}, u32[]{:S(2)}, u32[]{:S(2)}) %collective-permute-start.7) | collective-permute-done | bytes 1056 | tf_op jit(solution)/shard_map/ppermute | solution.py:296
  37.9 8.1 %collective-permute-done.6.far_ref = f32[264,256]{1,0:T(8,128)S(1)} collective-permute-done((f32[264,256]{1,0:T(8,128)S(1)}, f32[264,256]{1,0:T(8,128)S(1)}, u32[]{:S(2)}, u32[]{:S(2)}) %collective-permute-start.6) | collective-permute-done | bytes 270368 | tf_op jit(solution)/shard_map/ppermute | solution.py:309
  46.0 1.5 %last.1 = (f32[256,256]{1,0:T(8,128)}, f32[256,256]{1,0:T(8,128)}, f32[256,256]{1,0:T(8,128)}) custom-call(f32[264,256]{1,0:T(8,128)S(1)} %near.1.near_ref, f32[264,256]{1,0:T(8,128)S(1)} %collective-permute-done.6.far_ref, f32[256,256]{1,0:T(8,128)S(1)} %get-tuple-element.22.weight_ref, f32[256,1]{1,0:T(8,128)S(1)} %get-tuple-element.23.branch_ref, ...), custom_call_target="tpu_custom_call" | custom-call | flops 201326592 | bytes 2359296 | tf_op jit(solution)/shard_map/last/pallas_call | solution.py:259
  (1 shorter events, 0.0 us)
Async XLA Ops:
  2.9 26.5 %collective-permute-start.4 = (f32[3,256,256]{2,1,0:T(8,128)}, f32[3,256,256]{2,1,0:T(8,128)S(1)}, u32[]{:S(2)}, u32[]{:S(2)}) collective-permute-start(f32[3,256,256]{2,1,0:T(8,128)} %get-tuple-element.19), channel_id=1, source_target_pairs={{0,5},{1,4},{2,7},{3,6},{4,8},{5,9},{6,11},{7,10},{16,21},{17,20},... | collective-permute-start | bytes 2359304 | tf_op jit(solution)/shard_map/ppermute | solution.py:291
  7.3 22.1 %copy-start = (f32[1,1,7,256,256]{4,3,2,1,0:T(8,128)S(1)}, f32[1,1,7,256,256]{4,3,2,1,0:T(8,128)}, u32[]{:S(2)}) copy-start(f32[1,1,7,256,256]{4,3,2,1,0:T(8,128)} %param.9) | copy-start | bytes 5505028
  7.3 22.1 %copy-start.4 = (s32[7,16]{1,0:T(8,128)S(1)}, s32[7,16]{1,0:T(8,128)}, u32[]{:S(2)}) copy-start(s32[7,16]{1,0:T(8,128)} %constant.7.clone.table_ref) | copy-start | bytes 1348
  7.3 21.5 %collective-permute-start = (f32[2,256,256]{2,1,0:T(8,128)}, f32[2,256,256]{2,1,0:T(8,128)S(1)}, u32[]{:S(2)}, u32[]{:S(2)}) collective-permute-start(f32[2,256,256]{2,1,0:T(8,128)} %get-tuple-element.15), channel_id=1, source_target_pairs={{7,5},{3,1},{6,4},{4,2},{9,7},{8,6},{12,11},{13,10},{23,21},{19,17... | collective-permute-start | bytes 1572872 | tf_op jit(solution)/shard_map/ppermute | solution.py:294
  9.2 20.2 %collective-permute-start.1 = (f32[2,256,256]{2,1,0:T(8,128)}, f32[2,256,256]{2,1,0:T(8,128)S(1)}, u32[]{:S(2)}, u32[]{:S(2)}) collective-permute-start(f32[2,256,256]{2,1,0:T(8,128)} %get-tuple-element.16), channel_id=1, source_target_pairs={{2,0},{6,5},{5,4},{3,2},{8,7},{7,6},{10,3},{11,8},{12,9},{9,11},{1... | collective-permute-start | bytes 1572872 | tf_op jit(solution)/shard_map/ppermute | solution.py:294
  10.5 18.3 %collective-permute-start.2 = (f32[1,256,256]{2,1,0:T(8,128)}, f32[1,256,256]{2,1,0:T(8,128)S(1)}, u32[]{:S(2)}, u32[]{:S(2)}) collective-permute-start(f32[1,256,256]{2,1,0:T(8,128)} %get-tuple-element.17), channel_id=1, source_target_pairs={{3,0},{7,1},{5,2},{4,3},{9,8},{8,9},{10,6},{13,11},{11,10},{14,7},... | collective-permute-start | bytes 786440 | tf_op jit(solution)/shard_map/ppermute | solution.py:294
  11.8 22.7 %collective-permute-start.3 = (f32[1,256,256]{2,1,0:T(8,128)}, f32[1,256,256]{2,1,0:T(8,128)}, u32[]{:S(2)}, u32[]{:S(2)}) collective-permute-start(f32[1,256,256]{2,1,0:T(8,128)} %get-tuple-element.18), channel_id=1, source_target_pairs={{4,0},{8,1},{6,2},{5,3},{7,4},{10,5},{11,6},{20,16},{24,17},{22,18... | collective-permute-start | bytes 786440 | tf_op jit(solution)/shard_map/ppermute | solution.py:294
  13.9 16.2 %copy-start.7 = (f32[1,256,256]{2,1,0:T(8,128)S(1)}, f32[1,256,256]{2,1,0:T(8,128)}, u32[]{:S(2)}) copy-start(f32[1,256,256]{2,1,0:T(8,128)} %pick_late.1) | copy-start | bytes 786436
  13.9 17.6 %copy-start.5 = (s32[1,1,256]{2,1,0:T(1,128)S(1)}, s32[1,1,256]{2,1,0:T(1,128)}, u32[]{:S(2)}) copy-start(s32[1,1,256]{2,1,0:T(1,128)} %param.11) | copy-start | bytes 3076
  13.9 20.2 %copy-start.8 = (f32[64]{0:T(128)S(1)}, f32[64]{0:T(128)}, u32[]{:S(2)}) copy-start(f32[64]{0:T(128)} %param.13) | copy-start | bytes 772
  13.9 20.3 %copy-start.2 = (f32[1,1,7,256,256]{4,3,2,1,0:T(8,128)S(1)}, f32[1,1,7,256,256]{4,3,2,1,0:T(8,128)}, u32[]{:S(2)}) copy-start(f32[1,1,7,256,256]{4,3,2,1,0:T(8,128)} %param.10) | copy-start | bytes 5505028
  13.9 20.3 %copy-start.3 = (s32[1,1,256,256]{3,2,1,0:T(8,128)S(1)}, s32[1,1,256,256]{3,2,1,0:T(8,128)}, u32[]{:S(2)}) copy-start(s32[1,1,256,256]{3,2,1,0:T(8,128)} %param.12) | copy-start | bytes 786436
  30.1 4.4 %copy-start.1 = (f32[1,1,7,256,256]{4,3,2,1,0:T(8,128)S(1)}, f32[1,1,7,256,256]{4,3,2,1,0:T(8,128)}, u32[]{:S(2)}) copy-start(f32[1,1,7,256,256]{4,3,2,1,0:T(8,128)} %param.8) | copy-start | bytes 5505028
  30.1 4.4 %copy-start.6 = (s32[7,16]{1,0:T(8,128)S(1)}, s32[7,16]{1,0:T(8,128)}, u32[]{:S(2)}) copy-start(s32[7,16]{1,0:T(8,128)} %constant.8.clone.table_ref) | copy-start | bytes 1348
  30.1 4.4 %collective-permute-start.5 = (f32[1,256,256]{2,1,0:T(8,128)S(1)}, f32[1,256,256]{2,1,0:T(8,128)S(1)}, u32[]{:S(2)}, u32[]{:S(2)}) collective-permute-start(f32[1,256,256]{2,1,0:T(8,128)S(1)} %copy-done.7), channel_id=1, source_target_pairs={{1,0},{2,1},{9,3},{10,4},{11,5},{12,7},{17,16},{18,17},{25,19},{26... | collective-permute-start | bytes 786440 | tf_op jit(solution)/shard_map/ppermute | solution.py:310
  31.5 6.4 %collective-permute-start.7 = (s32[1,256]{1,0:T(1,128)S(1)}, s32[1,256]{1,0:T(1,128)S(1)}, u32[]{:S(2)}, u32[]{:S(2)}) collective-permute-start(s32[1,256]{1,0:T(1,128)S(1)} %bitcast.18), channel_id=1, source_target_pairs={{8,0},{9,1},{10,2},{11,3},{12,4},{13,5},{14,6},{15,7},{24,16},{25,... | collective-permute-start | bytes 3080 | tf_op jit(solution)/shard_map/ppermute | solution.py:296
  32.8 13.2 %collective-permute-start.6 = (f32[264,256]{1,0:T(8,128)S(1)}, f32[264,256]{1,0:T(8,128)S(1)}, u32[]{:S(2)}, u32[]{:S(2)}) collective-permute-start(f32[264,256]{1,0:T(8,128)S(1)} %far.1), channel_id=1, source_target_pairs={{5,0},{4,1},{7,2},{6,3},{8,4},{9,5},{11,6},{10,7},{21,16},{20,17},... | collective-permute-start | bytes 811016 | tf_op jit(solution)/shard_map/ppermute | solution.py:309

commit v5 on v4

--- a/solution.py
+++ b/solution.py
@@ -14,14 +14,14 @@
 FIRST = 1
 LATE = 4
 PLAN = (
-    (5, (5, 6, 7), (4, 1, 2, 3, -1, 1, 0)),
-    (3, (3, 4, 5), (4, 0, -1, 1, 0, 2, 3)),
-    (5, (5, 6, 7), (1, 0, 2, 3, -1, 1, 0)),
-    (3, (3, 4, 5), (2, 3, -1, 1, 0, 4, 1)),
-    (4, (4, 5, 7), (1, 0, 3, -1, 2, 4, 1)),
-    (4, (3, 4, 7), (1, 0, 2, -1, 3, 4, 1)),
-    (5, (3, 6, 7), (1, 0, 1, 2, 3, 0, 2)),
-    (3, (3, 4, 6), (1, 0, -1, 2, 4, 0, 2)),
+    (5, (5, 6, 7), (1, 4, 2, 3, -1, 0, 1)),
+    (3, (3, 4, 5), (1, 0, -1, 0, 1, 2, 3)),
+    (5, (5, 6, 7), (1, 0, 2, 3, -1, 0, 1)),
+    (3, (3, 4, 5), (2, 3, -1, 0, 1, 4, 1)),
+    (4, (4, 5, 7), (0, 1, 3, -1, 2, 4, 0)),
+    (4, (3, 4, 7), (0, 1, 2, -1, 3, 4, 0)),
+    (5, (3, 6, 7), (0, 1, 0, 2, 3, 1, 2)),
+    (3, (3, 4, 6), (0, 1, -1, 2, 4, 1, 2)),
 )
 
 

time: 47.9 us -> 47.5 us (level)
  the two profiles are of different devices: /device:TPU:0 before, /device:TPU:13 now
where the time goes in v5:
time: 47.5 us; the launch traced here: 47.2 us
  starting transfers between devices  18.6 us (39%)
  waiting for transfers between devices  16.6 us (35%)
  Pallas kernels  11 us (23%)
  between operations  0.86 us (2%)
    ppermute x4, starting transfers between devices, per_device(): rights = {t: lax.ppermute(blocks[t], 'row', plan.pairs[t]) for t in early}  11.4 us
    pallas_call x7, Pallas kernels, call(): pl.pallas_call(kernel, out_shape=outs, in_specs=ins, out_specs=(vmem,) *...  11 us
    ppermute x4, waiting for transfers between devices, per_device(): rights = {t: lax.ppermute(blocks[t], 'row', plan.pairs[t]) for t in early}  7.59 us
    ppermute x1, waiting for transfers between devices, per_device(): lax.ppermute(block, 'row', plan.pairs[t])  4.68 us
    ppermute x1, waiting for transfers between devices, per_device(): far = lax.ppermute(far, 'row', plan.back)  4.37 us
    ppermute x1, starting transfers between devices, per_device(): left = lax.ppermute(left, 'row', plan.there)  2.52 us
    ppermute x1, starting transfers between devices, per_device(): far = lax.ppermute(far, 'row', plan.back)  1.92 us
    ppermute x1, starting transfers between devices, per_device(): lax.ppermute(block, 'row', plan.pairs[t])  1.42 us
  transfers between devices with their start and end apart: 8, of which 4 were waited for; matrix products, arithmetic and copies ran while one was open for 0% of the time, Pallas kernels for 15%

profile of v5, /device:TPU:13, one launch (start us, length us, event | category | flops | bytes accessed | tf_op | source)
XLA Modules:
  0.0 47.2 jit_solution(4311520392637610122)
XLA Ops:
  0.6 2.4 %pick_first.1 = (f32[3,256,256]{2,1,0:T(8,128)}, f32[2,256,256]{2,1,0:T(8,128)}) custom-call(f32[7,256,256]{2,1,0:T(8,128)} %bitcast.14, f32[7,256,256]{2,1,0:T(8,128)} %bitcast.10), custom_call_target="tpu_custom_call" | custom-call | bytes 2359296 | tf_op jit(solution)/shard_map/pick_first/pallas_call | solution.py:259
  3.1 2.5 %collective-permute-start.4 = (f32[3,256,256]{2,1,0:T(8,128)}, f32[3,256,256]{2,1,0:T(8,128)S(1)}, u32[]{:S(2)}, u32[]{:S(2)}) collective-permute-start(f32[3,256,256]{2,1,0:T(8,128)} %get-tuple-element.19), channel_id=1, source_target_pairs={{0,5},{1,4},{2,7},{3,6},{4,8},{5,9},{6,11},{7,10},{16,21},{17,20},... | collective-permute-start | bytes 2359304 | tf_op jit(solution)/shard_map/ppermute | solution.py:291
  5.6 0.0 copy-start
  5.6 0.0 copy-start.4
  5.6 2.8 %collective-permute-start = (f32[2,256,256]{2,1,0:T(8,128)}, f32[2,256,256]{2,1,0:T(8,128)S(1)}, u32[]{:S(2)}, u32[]{:S(2)}) collective-permute-start(f32[2,256,256]{2,1,0:T(8,128)} %get-tuple-element.15), channel_id=1, source_target_pairs={{6,5},{3,1},{5,4},{4,2},{8,7},{7,6},{11,8},{12,9},{9,11},{22,21},{... | collective-permute-start | bytes 1572872 | tf_op jit(solution)/shard_map/ppermute | solution.py:294
  8.4 2.2 %pick_rest.1 = (f32[2,256,256]{2,1,0:T(8,128)}, f32[1,256,256]{2,1,0:T(8,128)}, f32[1,256,256]{2,1,0:T(8,128)}) custom-call(f32[7,256,256]{2,1,0:T(8,128)} %bitcast.11), custom_call_target="tpu_custom_call" | custom-call | bytes 2359296 | tf_op jit(solution)/shard_map/pick_rest/pallas_call | solution.py:259
  10.6 2.6 %collective-permute-start.1 = (f32[2,256,256]{2,1,0:T(8,128)}, f32[2,256,256]{2,1,0:T(8,128)S(1)}, u32[]{:S(2)}, u32[]{:S(2)}) collective-permute-start(f32[2,256,256]{2,1,0:T(8,128)} %get-tuple-element.16), channel_id=1, source_target_pairs={{1,0},{7,5},{2,1},{6,4},{3,2},{9,7},{8,6},{10,3},{12,11},{13,10},{... | collective-permute-start | bytes 1572872 | tf_op jit(solution)/shard_map/ppermute | solution.py:294
  13.3 1.9 %collective-permute-start.2 = (f32[1,256,256]{2,1,0:T(8,128)}, f32[1,256,256]{2,1,0:T(8,128)S(1)}, u32[]{:S(2)}, u32[]{:S(2)}) collective-permute-start(f32[1,256,256]{2,1,0:T(8,128)} %get-tuple-element.17), channel_id=1, source_target_pairs={{3,0},{7,1},{5,2},{4,3},{9,8},{8,9},{10,6},{13,11},{11,10},{14,7},... | collective-permute-start | bytes 786440 | tf_op jit(solution)/shard_map/ppermute | solution.py:294
  15.2 4.1 %collective-permute-start.3 = (f32[1,256,256]{2,1,0:T(8,128)}, f32[1,256,256]{2,1,0:T(8,128)}, u32[]{:S(2)}, u32[]{:S(2)}) collective-permute-start(f32[1,256,256]{2,1,0:T(8,128)} %get-tuple-element.18), channel_id=1, source_target_pairs={{4,0},{8,1},{6,2},{5,3},{7,4},{10,5},{11,6},{20,16},{24,17},{22,18... | collective-permute-start | bytes 786440 | tf_op jit(solution)/shard_map/ppermute | solution.py:294
  19.3 0.7 %pick_late.1 = f32[1,256,256]{2,1,0:T(8,128)} custom-call(f32[7,256,256]{2,1,0:T(8,128)} %bitcast.12), custom_call_target="tpu_custom_call" | custom-call | bytes 2359296 | tf_op jit(solution)/shard_map/pick_late/pallas_call | solution.py:259
  20.0 0.0 copy-start.7
  20.0 0.0 copy-start.5
  20.0 0.0 copy-start.8
  20.0 0.0 copy-start.2
  20.1 0.0 copy-start.3
  20.1 6.2 %collective-permute-done.2.refs_2_ = f32[1,256,256]{2,1,0:T(8,128)S(1)} collective-permute-done((f32[1,256,256]{2,1,0:T(8,128)}, f32[1,256,256]{2,1,0:T(8,128)S(1)}, u32[]{:S(2)}, u32[]{:S(2)}) %collective-permute-start.2) | collective-permute-done | bytes 262176 | tf_op jit(solution)/shard_map/ppermute | solution.py:294
  26.3 0.0 collective-permute-done.refs_0_
  26.3 1.4 %collective-permute-done.1.refs_1_ = f32[2,256,256]{2,1,0:T(8,128)S(1)} collective-permute-done((f32[2,256,256]{2,1,0:T(8,128)}, f32[2,256,256]{2,1,0:T(8,128)S(1)}, u32[]{:S(2)}, u32[]{:S(2)}) %collective-permute-start.1) | collective-permute-done | bytes 524320 | tf_op jit(solution)/shard_map/ppermute | solution.py:294
  27.6 0.0 collective-permute-done.4.left_ref
  27.6 0.0 copy-done
  27.7 0.0 copy-done.4
  27.7 1.6 %far.1 = f32[264,256]{1,0:T(8,128)S(1)} custom-call(s32[7,16]{1,0:T(8,128)S(1)} %copy-done.4, f32[7,256,256]{2,1,0:T(8,128)S(1)} %bitcast.13, f32[3,256,256]{2,1,0:T(8,128)S(1)} %collective-permute-done.4.left_ref, f32[2,256,256]{2,1,0:T(8,128)S(1)} %collective-permute-done.refs_0_, f32[2,256,256]{2,1,0:T(8,128)S(1)} %collective-permute-done.1.refs_1_, ...), custom_call_target="tpu_custom_call" | custom-call | flops 301989888 | bytes 2359296 | tf_op jit(solution)/shard_map/far/pallas_call | solution.py:259
  29.2 0.0 copy-done.7
  29.3 0.0 copy-start.1
  29.3 0.0 copy-start.6
  29.3 1.4 %collective-permute-start.5 = (f32[1,256,256]{2,1,0:T(8,128)S(1)}, f32[1,256,256]{2,1,0:T(8,128)S(1)}, u32[]{:S(2)}, u32[]{:S(2)}) collective-permute-start(f32[1,256,256]{2,1,0:T(8,128)S(1)} %copy-done.7), channel_id=1, source_target_pairs={{2,0},{9,3},{10,4},{11,5},{12,7},{18,16},{25,19},{26,20},{27,21},{... | collective-permute-start | bytes 786440 | tf_op jit(solution)/shard_map/ppermute | solution.py:310
  30.7 0.0 copy-done.5
  30.7 1.3 %collective-permute-start.7 = (s32[1,256]{1,0:T(1,128)S(1)}, s32[1,256]{1,0:T(1,128)S(1)}, u32[]{:S(2)}, u32[]{:S(2)}) collective-permute-start(s32[1,256]{1,0:T(1,128)S(1)} %bitcast.18), channel_id=1, source_target_pairs={{8,0},{9,1},{10,2},{11,3},{12,4},{13,5},{14,6},{15,7},{24,16},{25,... | collective-permute-start | bytes 3080 | tf_op jit(solution)/shard_map/ppermute | solution.py:296
  32.0 1.9 %collective-permute-start.6 = (f32[264,256]{1,0:T(8,128)S(1)}, f32[264,256]{1,0:T(8,128)S(1)}, u32[]{:S(2)}, u32[]{:S(2)}) collective-permute-start(f32[264,256]{1,0:T(8,128)S(1)} %far.1), channel_id=1, source_target_pairs={{5,0},{4,1},{7,2},{6,3},{8,4},{9,5},{11,6},{10,7},{21,16},{20,17},... | collective-permute-start | bytes 811016 | tf_op jit(solution)/shard_map/ppermute | solution.py:309
  33.9 0.0 copy-done.8
  34.0 0.0 copy-done.2
  34.0 0.0 copy-done.3
  34.0 0.3 weights.1
  34.3 0.0 collective-permute-done.3.refs_3_
  34.3 4.7 %collective-permute-done.5.refs_4_ = f32[1,256,256]{2,1,0:T(8,128)S(1)} collective-permute-done((f32[1,256,256]{2,1,0:T(8,128)S(1)}, f32[1,256,256]{2,1,0:T(8,128)S(1)}, u32[]{:S(2)}, u32[]{:S(2)}) %collective-permute-start.5) | collective-permute-done | bytes 262176 | tf_op jit(solution)/shard_map/ppermute | solution.py:310
  39.0 0.0 copy-done.1
  39.0 0.0 copy-done.6
  39.0 2.3 %near.1.near_ref = f32[264,256]{1,0:T(8,128)S(1)} custom-call(s32[7,16]{1,0:T(8,128)S(1)} %copy-done.6, f32[7,256,256]{2,1,0:T(8,128)S(1)} %bitcast.15, f32[2,256,256]{2,1,0:T(8,128)S(1)} %collective-permute-done.refs_0_, f32[2,256,256]{2,1,0:T(8,128)S(1)} %collective-permute-done.1.refs_1_, f32[1,256,256]{2,1,0:T(8,128)S(1)} %collective-permute-done.2.refs_2_, ...), custom_call_target="tpu_custom_call" | custom-call | flops 2013265920 | bytes 2359296 | tf_op jit(solution)/shard_map/near/pallas_call | solution.py:259
  41.3 0.0 collective-permute-done.7.end_ref
  41.3 4.4 %collective-permute-done.6.far_ref = f32[264,256]{1,0:T(8,128)S(1)} collective-permute-done((f32[264,256]{1,0:T(8,128)S(1)}, f32[264,256]{1,0:T(8,128)S(1)}, u32[]{:S(2)}, u32[]{:S(2)}) %collective-permute-start.6) | collective-permute-done | bytes 270368 | tf_op jit(solution)/shard_map/ppermute | solution.py:309
  45.7 1.5 %last.1 = (f32[256,256]{1,0:T(8,128)}, f32[256,256]{1,0:T(8,128)}, f32[256,256]{1,0:T(8,128)}) custom-call(f32[264,256]{1,0:T(8,128)S(1)} %near.1.near_ref, f32[264,256]{1,0:T(8,128)S(1)} %collective-permute-done.6.far_ref, f32[256,256]{1,0:T(8,128)S(1)} %get-tuple-element.22.weight_ref, f32[256,1]{1,0:T(8,128)S(1)} %get-tuple-element.23.branch_ref, ...), custom_call_target="tpu_custom_call" | custom-call | flops 201326592 | bytes 2359296 | tf_op jit(solution)/shard_map/last/pallas_call | solution.py:259
  (1 shorter events, 0.0 us)
Async XLA Ops:
  3.1 24.6 %collective-permute-start.4 = (f32[3,256,256]{2,1,0:T(8,128)}, f32[3,256,256]{2,1,0:T(8,128)S(1)}, u32[]{:S(2)}, u32[]{:S(2)}) collective-permute-start(f32[3,256,256]{2,1,0:T(8,128)} %get-tuple-element.19), channel_id=1, source_target_pairs={{0,5},{1,4},{2,7},{3,6},{4,8},{5,9},{6,11},{7,10},{16,21},{17,20},... | collective-permute-start | bytes 2359304 | tf_op jit(solution)/shard_map/ppermute | solution.py:291
  5.6 22.1 %copy-start = (f32[1,1,7,256,256]{4,3,2,1,0:T(8,128)S(1)}, f32[1,1,7,256,256]{4,3,2,1,0:T(8,128)}, u32[]{:S(2)}) copy-start(f32[1,1,7,256,256]{4,3,2,1,0:T(8,128)} %param.9) | copy-start | bytes 5505028
  5.6 22.1 %copy-start.4 = (s32[7,16]{1,0:T(8,128)S(1)}, s32[7,16]{1,0:T(8,128)}, u32[]{:S(2)}) copy-start(s32[7,16]{1,0:T(8,128)} %constant.7.clone.table_ref) | copy-start | bytes 1348
  5.6 20.7 %collective-permute-start = (f32[2,256,256]{2,1,0:T(8,128)}, f32[2,256,256]{2,1,0:T(8,128)S(1)}, u32[]{:S(2)}, u32[]{:S(2)}) collective-permute-start(f32[2,256,256]{2,1,0:T(8,128)} %get-tuple-element.15), channel_id=1, source_target_pairs={{6,5},{3,1},{5,4},{4,2},{8,7},{7,6},{11,8},{12,9},{9,11},{22,21},{... | collective-permute-start | bytes 1572872 | tf_op jit(solution)/shard_map/ppermute | solution.py:294
  10.6 17.0 %collective-permute-start.1 = (f32[2,256,256]{2,1,0:T(8,128)}, f32[2,256,256]{2,1,0:T(8,128)S(1)}, u32[]{:S(2)}, u32[]{:S(2)}) collective-permute-start(f32[2,256,256]{2,1,0:T(8,128)} %get-tuple-element.16), channel_id=1, source_target_pairs={{1,0},{7,5},{2,1},{6,4},{3,2},{9,7},{8,6},{10,3},{12,11},{13,10},{... | collective-permute-start | bytes 1572872 | tf_op jit(solution)/shard_map/ppermute | solution.py:294
  13.3 13.0 %collective-permute-start.2 = (f32[1,256,256]{2,1,0:T(8,128)}, f32[1,256,256]{2,1,0:T(8,128)S(1)}, u32[]{:S(2)}, u32[]{:S(2)}) collective-permute-start(f32[1,256,256]{2,1,0:T(8,128)} %get-tuple-element.17), channel_id=1, source_target_pairs={{3,0},{7,1},{5,2},{4,3},{9,8},{8,9},{10,6},{13,11},{11,10},{14,7},... | collective-permute-start | bytes 786440 | tf_op jit(solution)/shard_map/ppermute | solution.py:294
  15.2 19.1 %collective-permute-start.3 = (f32[1,256,256]{2,1,0:T(8,128)}, f32[1,256,256]{2,1,0:T(8,128)}, u32[]{:S(2)}, u32[]{:S(2)}) collective-permute-start(f32[1,256,256]{2,1,0:T(8,128)} %get-tuple-element.18), channel_id=1, source_target_pairs={{4,0},{8,1},{6,2},{5,3},{7,4},{10,5},{11,6},{20,16},{24,17},{22,18... | collective-permute-start | bytes 786440 | tf_op jit(solution)/shard_map/ppermute | solution.py:294
  20.0 9.2 %copy-start.7 = (f32[1,256,256]{2,1,0:T(8,128)S(1)}, f32[1,256,256]{2,1,0:T(8,128)}, u32[]{:S(2)}) copy-start(f32[1,256,256]{2,1,0:T(8,128)} %pick_late.1) | copy-start | bytes 786436
  20.0 10.7 %copy-start.5 = (s32[1,1,256]{2,1,0:T(1,128)S(1)}, s32[1,1,256]{2,1,0:T(1,128)}, u32[]{:S(2)}) copy-start(s32[1,1,256]{2,1,0:T(1,128)} %param.11) | copy-start | bytes 3076
  20.0 13.9 %copy-start.8 = (f32[64]{0:T(128)S(1)}, f32[64]{0:T(128)}, u32[]{:S(2)}) copy-start(f32[64]{0:T(128)} %param.13) | copy-start | bytes 772
  20.0 13.9 %copy-start.2 = (f32[1,1,7,256,256]{4,3,2,1,0:T(8,128)S(1)}, f32[1,1,7,256,256]{4,3,2,1,0:T(8,128)}, u32[]{:S(2)}) copy-start(f32[1,1,7,256,256]{4,3,2,1,0:T(8,128)} %param.10) | copy-start | bytes 5505028
  20.1 13.9 %copy-start.3 = (s32[1,1,256,256]{3,2,1,0:T(8,128)S(1)}, s32[1,1,256,256]{3,2,1,0:T(8,128)}, u32[]{:S(2)}) copy-start(s32[1,1,256,256]{3,2,1,0:T(8,128)} %param.12) | copy-start | bytes 786436
  29.3 9.7 %copy-start.1 = (f32[1,1,7,256,256]{4,3,2,1,0:T(8,128)S(1)}, f32[1,1,7,256,256]{4,3,2,1,0:T(8,128)}, u32[]{:S(2)}) copy-start(f32[1,1,7,256,256]{4,3,2,1,0:T(8,128)} %param.8) | copy-start | bytes 5505028
  29.3 9.7 %copy-start.6 = (s32[7,16]{1,0:T(8,128)S(1)}, s32[7,16]{1,0:T(8,128)}, u32[]{:S(2)}) copy-start(s32[7,16]{1,0:T(8,128)} %constant.8.clone.table_ref) | copy-start | bytes 1348
  29.3 9.7 %collective-permute-start.5 = (f32[1,256,256]{2,1,0:T(8,128)S(1)}, f32[1,256,256]{2,1,0:T(8,128)S(1)}, u32[]{:S(2)}, u32[]{:S(2)}) collective-permute-start(f32[1,256,256]{2,1,0:T(8,128)S(1)} %copy-done.7), channel_id=1, source_target_pairs={{2,0},{9,3},{10,4},{11,5},{12,7},{18,16},{25,19},{26,20},{27,21},{... | collective-permute-start | bytes 786440 | tf_op jit(solution)/shard_map/ppermute | solution.py:310
  30.7 10.6 %collective-permute-start.7 = (s32[1,256]{1,0:T(1,128)S(1)}, s32[1,256]{1,0:T(1,128)S(1)}, u32[]{:S(2)}, u32[]{:S(2)}) collective-permute-start(s32[1,256]{1,0:T(1,128)S(1)} %bitcast.18), channel_id=1, source_target_pairs={{8,0},{9,1},{10,2},{11,3},{12,4},{13,5},{14,6},{15,7},{24,16},{25,... | collective-permute-start | bytes 3080 | tf_op jit(solution)/shard_map/ppermute | solution.py:296
  32.0 13.6 %collective-permute-start.6 = (f32[264,256]{1,0:T(8,128)S(1)}, f32[264,256]{1,0:T(8,128)S(1)}, u32[]{:S(2)}, u32[]{:S(2)}) collective-permute-start(f32[264,256]{1,0:T(8,128)S(1)} %far.1), channel_id=1, source_target_pairs={{5,0},{4,1},{7,2},{6,3},{8,4},{9,5},{11,6},{10,7},{21,16},{20,17},... | collective-permute-start | bytes 811016 | tf_op jit(solution)/shard_map/ppermute | solution.py:309
